TPU v7x, 512 devices: a whole 4x4x16 slice. The times are simulated.
512 devices in a mesh: seq: 32 (over x_lo, z), exp: 8 (over y, core), batch: 2 (over x_hi).
Axes of the slice: x: 4 (x_hi: 2, x_lo: 2; x = x_hi * 2 + x_lo), y: 4, z: 16, core: 2. Of those that a mesh axis runs over, the one named last changes fastest.
Arguments:
- queries: bfloat16 [2, 4096, 2048], P('batch', 'seq', 'exp'), may hold values from -100 to 100
- keys_values: bfloat16 [2, 4096, 1024], P('batch', 'seq', 'exp'), may hold values from -10 to 10
- sinks: float32 [32], P('exp'), may hold values from -1 to 4
- out_weight: bfloat16 [2048, 2880], P('exp'), may hold values from -0.25 to 0.25
- hidden_in: bfloat16 [2, 4096, 2880], P('batch', ('seq', 'exp')), may hold values from -3 to 3
- norm_gain: float32 [2880], replicated, may hold values from 0.1 to 1.9
- expert_ids: int32 [2, 4096, 4], P('batch', 'seq'), may hold values from 0 to 31, all different within a row; in each aligned block of 128 rows (0 to 127, 128 to 255, ..., all dimensions but the last counted through in order) at most 24 rows name the same one
- expert_gates: bfloat16 [2, 4096, 4], P('batch', 'seq'), may hold values from 0.099609375 to 0.59765625
- gate_weight: bfloat16 [32, 2880, 1440], P('seq', None, 'exp'), may hold values from -0.109375 to 0.109375
- up_weight: bfloat16 [32, 2880, 1440], P('seq', None, 'exp'), may hold values from -0.109375 to 0.109375
- down_weight: bfloat16 [32, 1440, 2880], P('seq', 'exp'), may hold values from -0.15625 to 0.15625
Outputs:
- layer_out: bfloat16 [2, 4096, 2880], P('batch', ('seq', 'exp'))
Inputs may be any that keep to these rules, and one draw needn't show every extreme that they name: `expert_ids`: each token names 4 different experts. In each block of 128 positions of a sequence no expert is named by more than 24 tokens, and in some block one expert is named by exactly 24.
All inputs are finite; a program needn't handle non-finite values.
Results may differ from a plain program's by a relative error of at most 0.015.
Values may be sent and summed in bfloat16 or wider, within the bound.
No kernel may reach another device: no remote copies, remote signals or barrier semaphores. Data moves between devices by JAX's collectives and lax.ppermute only.
A program may use at most 64 MiB of HBM per device.

v0:
```python
import jax
import jax.numpy as jnp
from jax import lax
from jax.sharding import PartitionSpec as P

HEAD = 64


def on_device(
    queries,
    keys_values,
    sinks,
    out_weight,
    hidden_in,
    norm_gain,
    expert_ids,
    expert_gates,
    gate_weight,
    up_weight,
    down_weight,
):
    seq_devices = lax.axis_size("seq")
    exp_devices = lax.axis_size("exp")
    block_rows = queries.shape[1]
    head_count = sinks.shape[0]
    kv_heads = keys_values.shape[2] // (2 * HEAD)
    group_size = head_count // kv_heads
    width = out_weight.shape[1]
    own_rows = hidden_in.shape[1]
    seq_rank = lax.axis_index("seq")
    exp_rank = lax.axis_index("exp")
    first_query = seq_rank * block_rows
    last_query = first_query + block_rows - 1
    query_grid = queries[0].reshape(block_rows, kv_heads, group_size, HEAD)
    sink_grid = sinks.reshape(kv_heads, group_size)[:, :, None]
    query_pos = first_query + jnp.arange(block_rows, dtype=jnp.int32)
    initial = (
        jnp.broadcast_to(sink_grid, (kv_heads, group_size, block_rows)),
        jnp.ones((kv_heads, group_size, block_rows), jnp.float32),
        jnp.zeros((kv_heads, group_size, block_rows, HEAD), jnp.float32),
    )
    shard_piece = lax.all_gather(keys_values, "seq", axis=1, tiled=True)

    def attend(state_in):
        running_max, running_sum, weighted = state_in
        piece_rows = shard_piece.shape[1]
        key_value = shard_piece[0].reshape(piece_rows, kv_heads, 2, HEAD)
        scores = (
            jnp.einsum(
                "ikgd,jkd->kgij",
                query_grid,
                key_value[:, :, 0, :],
                preferred_element_type=jnp.float32,
            )
            * 0.125
        )
        key_pos = jnp.arange(piece_rows, dtype=jnp.int32)
        scores = jnp.where(key_pos[None, :] <= query_pos[:, None], scores, -1e30)
        new_max = jnp.maximum(running_max, jnp.max(scores, axis=-1))
        rescale = jnp.exp(running_max - new_max)
        numerators = jnp.exp(scores - new_max[..., None])
        new_sum = running_sum * rescale + jnp.sum(numerators, axis=-1)
        update = jnp.einsum(
            "kgij,jkd->kgid",
            numerators.astype(jnp.bfloat16),
            key_value[:, :, 1, :],
            preferred_element_type=jnp.float32,
        )
        return (new_max, new_sum, weighted * rescale[..., None] + update)

    def keep_state(state_in):
        return state_in

    running_max, running_sum, weighted = lax.cond(
        jnp.int32(0) <= last_query, attend, keep_state, initial
    )
    mixed = (weighted / running_sum[..., None]).astype(jnp.bfloat16)
    heads_out = mixed.transpose(2, 0, 1, 3).reshape(block_rows, head_count * HEAD)
    first_row = exp_rank * own_rows
    head_term = jnp.dot(heads_out, out_weight, preferred_element_type=jnp.float32)
    placed = lax.dynamic_update_slice(
        jnp.zeros((block_rows, width), jnp.float32),
        hidden_in[0].astype(jnp.float32),
        (first_row, 0),
    )
    attention, stream_rows = lax.psum((head_term, placed), "exp")
    residual = (stream_rows + attention).astype(jnp.bfloat16)
    stream = residual.astype(jnp.float32)
    mean_square = jnp.mean(stream * stream, axis=-1, keepdims=True)
    normed = (stream * lax.rsqrt(mean_square + 1e-05) * norm_gain).astype(jnp.bfloat16)
    residual_own = lax.dynamic_slice_in_dim(residual, first_row, own_rows, 0)
    chosen = expert_ids[0]
    top_count = chosen.shape[1]
    capacity = exp_devices * (
        (3 * block_rows * top_count + 2 * seq_devices * exp_devices - 1)
        // (2 * seq_devices * exp_devices)
    )
    hits = (chosen[:, :, None] == jnp.arange(seq_devices, dtype=jnp.int32)).astype(jnp.int32)
    flat_hits = hits.reshape(block_rows * top_count, seq_devices)
    before = jnp.cumsum(flat_hits, axis=0) - flat_hits
    slot_index = jnp.sum(before * flat_hits, axis=1).reshape(block_rows, top_count)
    hit_float = hits.astype(jnp.float32)
    slot_hits = (slot_index[:, :, None] == jnp.arange(capacity, dtype=jnp.int32)).astype(
        jnp.float32
    )
    selector = jnp.einsum("tke,tkc->ect", hit_float, slot_hits).astype(jnp.bfloat16)
    outgoing = jnp.einsum(
        "ect,td->ecd", selector, normed, preferred_element_type=jnp.float32
    ).astype(jnp.bfloat16)
    arrived_rows = lax.all_to_all(outgoing, "seq", split_axis=0, concat_axis=0, tiled=True)
    gate = jnp.einsum(
        "scd,df->scf", arrived_rows, gate_weight[0], preferred_element_type=jnp.float32
    )
    lifted = jnp.einsum(
        "scd,df->scf", arrived_rows, up_weight[0], preferred_element_type=jnp.float32
    )
    returned = lax.all_to_all(
        jnp.einsum(
            "scf,fd->scd",
            (gate * jax.nn.sigmoid(1.702 * gate) * (lifted + 1.0)).astype(jnp.bfloat16),
            down_weight[0],
            preferred_element_type=jnp.float32,
        ).astype(jnp.bfloat16),
        "seq",
        split_axis=0,
        concat_axis=0,
        tiled=True,
    )
    slot_all = (slot_index[:, :, None] == jnp.arange(capacity, dtype=jnp.int32)).astype(jnp.float32)
    combiner = jnp.einsum(
        "tke,tkc,tk->tec", hit_float, slot_all, expert_gates[0].astype(jnp.float32)
    )
    combiner = combiner.reshape(block_rows, seq_devices * capacity).astype(jnp.bfloat16)
    returned_flat = returned.reshape(seq_devices * capacity, width)
    expert_sum = lax.psum_scatter(
        jnp.dot(combiner, returned_flat, preferred_element_type=jnp.float32),
        "exp",
        scatter_dimension=0,
        tiled=True,
    )
    layer_out = (residual_own.astype(jnp.float32) + expert_sum).astype(jnp.bfloat16)
    return layer_out[None]


def solution(mesh):
    placed = (
        P("batch", "seq", "exp"),
        P("batch", "seq", "exp"),
        P("exp"),
        P("exp", None),
        P("batch", ("seq", "exp"), None),
        P(),
        P("batch", "seq", None),
        P("batch", "seq", None),
        P("seq", None, "exp"),
        P("seq", None, "exp"),
        P("seq", "exp", None),
    )
    return jax.shard_map(
        on_device,
        mesh=mesh,
        in_specs=placed,
        out_specs=P("batch", ("seq", "exp"), None),
        check_vma=False,
    )
```

profile of v0, /device:TPU:2, one launch (start us, length us, event | category | flops | bytes accessed | tf_op | source)
XLA Modules:
  0.0 686.3 jit_solution(8327945657944251737)
XLA Ops:
  6.5 1.6 copy.34
  8.2 0.8 copy.38
  9.2 2.1 copy.36
  11.3 1.2 reduce-window.6
  13.0 0.8 copy.37
  13.7 1.4 fusion.17
  15.2 0.5 copy.42
  15.7 119.3 %all-gather.2.cloned.1.call-done = bf16[1,4096,128]{1,2,0:T(8,128)(2,1)} async-done(((bf16[1,128,128]{1,2,0:T(8,128)(2,1)}), bf16[1,4096,128]{1,2,0:T(8,128)(2,1)}) %all-gather.2.cloned.1.call-update) | async-done | bytes 1048592 | tf_op jit(solution)/shard_map/all_gather | solution.py:42
  135.0 5.6 conditional.1
  135.4 2.4 fusion.46
  137.9 1.4 fusion.9
  139.4 1.1 fusion.1
  140.6 0.5 fusion.47
  141.1 0.5 copy-done.2
  141.7 1.6 convert_add_fusion
  143.3 11.1 %dynamic-update-slice = f32[128,2880]{0,1:T(8,128)S(1)} dynamic-update-slice(f32[128,2880]{0,1:T(8,128)S(1)} %fusion.47, f32[16,2880]{0,1:T(8,128)} %convert_add_fusion, s32[]{:T(128)S(6)} %select_n.8, s32[]{:T(128)} %constant.22.clone.1) | dynamic-update-slice | bytes 368644 | tf_op jit(solution)/shard_map/add | solution.py:87
  154.4 52.7 %all-reduce.1 = bf16[128,2880]{0,1:T(8,128)(2,1)} all-reduce(f32[128,2880]{0,1:T(8,128)S(1)} %dynamic-update-slice), channel_id=1, replica_groups=mesh['seq'=32,'exp'=8,'batch'=2] {'exp'}, use_global_device_ids=true, to_apply=%region_0.0 | all-reduce | flops 368640 | bytes 2211840 | tf_op jit(solution)/shard_map/psum | solution.py:86
  207.1 1.5 fusion.14
  208.6 3.0 convolution_convert_fusion.1
  211.6 211.1 %all_to_all.10 = bf16[32,24,2880]{2,1,0:T(8,128)(2,1)S(1)} all-to-all(bf16[32,24,2880]{2,1,0:T(8,128)(2,1)S(1)} %convolution_convert_fusion.1), channel_id=1, replica_groups=mesh['seq'=32,'exp'=8,'batch'=2] {'seq'}, dimensions={0} | all-to-all | bytes 8847360 | tf_op jit(solution)/shard_map/all_to_all | solution.py:110
  422.7 1.4 fusion.22
  424.1 1.4 fusion.19
  425.6 1.4 convolution_convert_fusion
  427.0 3.5 copy.44
  430.4 6.2 all-to-all-start.1
  436.8 1.5 convolution_convert_fusion.3
  438.9 193.7 %all-to-all-done.1 = bf16[32,24,2880]{2,1,0:T(8,128)(2,1)} async-done(((bf16[32,24,2880]{2,1,0:T(8,128)(2,1)}), bf16[32,24,2880]{2,1,0:T(8,128)(2,1)}, u32[]{:S(2)}, u32[]{:S(2)}) %all-to-all-start.1) | async-done | bytes 4423712 | tf_op jit(solution)/shard_map/all_to_all | solution.py:117
  632.6 4.3 convolution_bitcast_fusion
  636.9 37.5 %reduce-scatter.4.cloned.1.call-done = f32[16,2880]{1,0:T(8,128)} async-done(((f32[128,2880]{1,0:T(8,128)}), f32[16,2880]{1,0:T(8,128)}) %reduce-scatter.4.cloned.1.call-update) | async-done | bytes 184336
  674.4 2.5 copy.56
  676.9 1.6 fusion.24
  678.5 0.9 copy.48
  (43 shorter events, 2.1 us)
Async XLA Ops:
  6.5 134.1 %copy-start = (bf16[256,2880]{0,1:T(8,128)(2,1)S(1)}, bf16[256,2880]{0,1:T(8,128)(2,1)}, u32[]{:S(2)}) copy-start(bf16[256,2880]{0,1:T(8,128)(2,1)} %param.16) | copy-start | bytes 4423684
  6.5 128.4 %all-gather.2.cloned.1.call-start = ((), (), s32[]{:S(2)}) async-start(), calls=%async_computation.3 | async-start | bytes 1081344 | tf_op jit(solution)/shard_map/all_gather | solution.py:42
  9.2 125.8 %copy-start.5 = (bf16[1,128,256]{2,1,0:T(8,128)(2,1)S(1)}, bf16[1,128,256]{2,1,0:T(8,128)(2,1)}, u32[]{:S(2)}) copy-start(bf16[1,128,256]{2,1,0:T(8,128)(2,1)} %param.13) | copy-start | bytes 196612
  9.2 125.8 %copy-start.7 = (f32[4]{0:T(128)S(1)}, f32[4]{0:T(128)}, u32[]{:S(2)}) copy-start(f32[4]{0:T(128)} %param.15) | copy-start | bytes 52
  135.4 2.5 copy-start.4
  140.6 1.1 copy-start.2
  154.4 54.2 %copy-start.6 = (f32[2880]{0:T(1024)S(1)}, f32[2880]{0:T(1024)}, u32[]{:S(2)}) copy-start(f32[2880]{0:T(1024)} %param.18) | copy-start | bytes 34564
  211.6 211.1 %copy-start.9 = (bf16[1,2880,180]{1,2,0:T(8,128)(2,1)S(1)}, bf16[1,2880,180]{1,2,0:T(8,128)(2,1)}, u32[]{:S(2)}) copy-start(bf16[1,2880,180]{1,2,0:T(8,128)(2,1)} %param.21) | copy-start | bytes 3110404
  422.7 1.4 copy-start.10
  424.1 1.4 copy-start.3
  430.4 6.2 copy-start.8
  430.4 202.2 %all-to-all-start.1 = ((bf16[32,24,2880]{2,1,0:T(8,128)(2,1)}), bf16[32,24,2880]{2,1,0:T(8,128)(2,1)}, u32[]{:S(2)}, u32[]{:S(2)}) async-start(bf16[32,24,2880]{2,1,0:T(8,128)(2,1)} %copy.44), calls=%async_computation.1 | async-start | bytes 9043968 | tf_op jit(solution)/shard_map/all_to_all | solution.py:117
  436.6 237.8 %reduce-scatter.4.cloned.1.call-start = ((), (), s32[]{:S(2)}) async-start(), calls=%async_computation.4 | async-start | bytes 1695744
  636.9 40.0 %copy-start.1 = (bf16[128,2880]{0,1:T(8,128)(2,1)S(1)}, bf16[128,2880]{0,1:T(8,128)(2,1)}, u32[]{:S(2)}) copy-start(bf16[128,2880]{0,1:T(8,128)(2,1)} %all-reduce.1) | copy-start | bytes 2211844
Sparse Core Ops, SparseCore 0:
  9.4 125.5 all-gather.1
  637.0 37.3 reduce-scatter.3
where the time goes:
time: 687 us; the launch traced here: 686 us
  waiting for transfers between devices  350 us (51%)
  blocking collectives  264 us (38%)
  local copies, waits for them, and re-layouts  25.6 us (4%)
  matrix products  18.8 us (3%)
  between operations  13.6 us (2%)
  other arithmetic  7.74 us (1%)
    all_to_all x1, blocking collectives, on_device(): lax.all_to_all(outgoing, 'seq', split_axis=0, concat_axis=0, tiled=True)  211 us
    all_to_all x1, waiting for transfers between devices, on_device(): lax.all_to_all(jnp.einsum('scf,fd->scd', (gate * jax.nn.sigmoid(1.702 * g...  194 us
    all_gather x1, waiting for transfers between devices, on_device(): shard_piece = lax.all_gather(keys_values, 'seq', axis=1, tiled=True)  119 us
    psum x1, blocking collectives, on_device(): attention, stream_rows = lax.psum((head_term, placed), 'exp')  52.7 us
    unnamed x3, waiting for transfers between devices  37.5 us
  transfers between devices with their start and end apart: 3, of which 3 were waited for; matrix products, arithmetic and copies ran while one was open for 1% of the time, Pallas kernels for 0%

commit v1 on v0

v1 whole, which is shorter than its diff:
```python
import functools

import jax
import jax.numpy as jnp
from jax import lax
from jax.experimental import pallas as pl
from jax.experimental.pallas import tpu as pltpu
from jax.sharding import PartitionSpec as P

HEAD = 64
HALF = 192


def expert_kernel(rows_ref, lift_ref, down_ref, out_ref, total_ref):
    step = pl.program_id(0)
    units = down_ref.shape[1]
    both = jnp.dot(rows_ref[...], lift_ref[0], preferred_element_type=jnp.float32)
    gate = both[:, :units]
    lifted = both[:, HALF : HALF + units]
    hidden = (gate * jax.nn.sigmoid(1.702 * gate) * (lifted + 1.0)).astype(jnp.bfloat16)
    term = jnp.dot(hidden, down_ref[0], preferred_element_type=jnp.float32)

    @pl.when(step == 0)
    def _():
        total_ref[...] = term

    @pl.when(step > 0)
    def _():
        total_ref[...] += term

    @pl.when(step == pl.num_programs(0) - 1)
    def _():
        out_ref[...] = total_ref[...].astype(out_ref.dtype)


def run_expert(rows, lift, down):
    count, width = rows.shape
    groups, units, _ = down.shape
    return pl.pallas_call(
        expert_kernel,
        grid=(groups,),
        in_specs=[
            pl.BlockSpec((count, width), lambda g: (0, 0)),
            pl.BlockSpec((1, width, 2 * HALF), lambda g: (g, 0, 0)),
            pl.BlockSpec((1, units, width), lambda g: (g, 0, 0)),
        ],
        out_specs=pl.BlockSpec((count, width), lambda g: (0, 0)),
        out_shape=jax.ShapeDtypeStruct((count, width), jnp.bfloat16),
        scratch_shapes=[pltpu.VMEM((count, width), jnp.float32)],
        compiler_params=pltpu.CompilerParams(vmem_limit_bytes=40 * 1024 * 1024),
        cost_estimate=pl.CostEstimate(
            flops=6 * count * width * units * groups,
            bytes_accessed=groups * (2 * HALF + units) * width * 2,
            transcendentals=count * units * groups,
        ),
    )(rows, lift, down)


def on_device(
    queries,
    keys_values,
    sinks,
    out_weight,
    hidden_in,
    norm_gain,
    expert_ids,
    expert_gates,
    gate_weight,
    up_weight,
    down_weight,
):
    seq_devices = lax.axis_size("seq")
    exp_devices = lax.axis_size("exp")
    block_rows = queries.shape[1]
    heads = sinks.shape[0]
    width = out_weight.shape[1]
    own_rows = hidden_in.shape[1]
    units = gate_weight.shape[2]
    seq_rank = lax.axis_index("seq")
    exp_rank = lax.axis_index("exp")

    with jax.named_scope("gather_weights"):
        zeros = jnp.zeros((width, HALF - units), jnp.bfloat16)
        lift_own = jnp.concatenate([gate_weight[0], zeros, up_weight[0], zeros], axis=1)
        lift_all = lax.all_gather(lift_own, "exp", axis=0, tiled=False)
        down_all = lax.all_gather(down_weight[0], "exp", axis=0, tiled=False)

    with jax.named_scope("gather_keys"):
        copies = jnp.broadcast_to(keys_values, (seq_devices,) + keys_values.shape[1:])
        pairs = lax.all_to_all(copies, "seq", split_axis=0, concat_axis=0, tiled=True)
        pairs = pairs.reshape(seq_devices * block_rows, 2 * HEAD)

    with jax.named_scope("attend"):
        grid = queries[0].reshape(block_rows, heads, HEAD)
        scores = (
            jnp.einsum("igd,jd->gij", grid, pairs[:, :HEAD], preferred_element_type=jnp.float32)
            * 0.125
        )
        query_pos = seq_rank * block_rows + jnp.arange(block_rows, dtype=jnp.int32)
        key_pos = jnp.arange(seq_devices * block_rows, dtype=jnp.int32)
        scores = jnp.where(key_pos[None, :] <= query_pos[:, None], scores, -1e30)
        largest = jnp.maximum(jnp.max(scores, axis=-1), sinks[:, None])
        numerators = jnp.exp(scores - largest[..., None])
        totals = jnp.sum(numerators, axis=-1) + jnp.exp(sinks[:, None] - largest)
        weighted = jnp.einsum(
            "gij,jd->gid",
            numerators.astype(jnp.bfloat16),
            pairs[:, HEAD:],
            preferred_element_type=jnp.float32,
        )
        mixed = (weighted / totals[..., None]).astype(jnp.bfloat16)
        heads_out = mixed.transpose(1, 0, 2).reshape(block_rows, heads * HEAD)

    with jax.named_scope("project"):
        head_term = jnp.dot(heads_out, out_weight, preferred_element_type=jnp.float32)
        head_parts = head_term.astype(jnp.bfloat16).reshape(exp_devices, own_rows, width)
        own_parts = lax.all_to_all(head_parts, "exp", split_axis=0, concat_axis=0, tiled=True)
        attention = jnp.sum(own_parts.astype(jnp.float32), axis=0)
        residual = (hidden_in[0].astype(jnp.float32) + attention).astype(jnp.bfloat16)

    with jax.named_scope("norm"):
        stream = residual.astype(jnp.float32)
        mean_square = jnp.mean(stream * stream, axis=-1, keepdims=True)
        normed_own = (stream * lax.rsqrt(mean_square + 1e-05) * norm_gain).astype(jnp.bfloat16)
        normed = lax.all_gather(normed_own, "exp", axis=0, tiled=True)

    with jax.named_scope("route"):
        chosen = expert_ids[0]
        top_count = chosen.shape[1]
        share = (3 * block_rows * top_count + 2 * seq_devices * exp_devices - 1) // (
            2 * seq_devices * exp_devices
        )
        hits = (chosen[:, :, None] == jnp.arange(seq_devices, dtype=jnp.int32)).astype(jnp.float32)
        token_hits = jnp.sum(hits, axis=1)
        earlier = (
            jnp.arange(block_rows)[:, None] > jnp.arange(block_rows)[None, :]
        ).astype(jnp.float32)
        slots = jnp.dot(earlier, token_hits)
        wanted = (exp_rank * share + jnp.arange(share, dtype=jnp.int32)).astype(jnp.float32)
        picks = (token_hits[:, :, None] > 0) & (slots[:, :, None] == wanted)
        selector = picks.astype(jnp.bfloat16)
        factor = jnp.einsum("tke,tk->te", hits, expert_gates[0].astype(jnp.float32))
        combiner = jnp.where(picks, factor[:, :, None], 0.0).astype(jnp.bfloat16)
        combiner = combiner.reshape(block_rows, seq_devices * share)

    with jax.named_scope("dispatch"):
        outgoing = jnp.einsum(
            "tec,td->ecd", selector, normed, preferred_element_type=jnp.float32
        ).astype(jnp.bfloat16)
        arrived = lax.all_to_all(outgoing, "seq", split_axis=0, concat_axis=0, tiled=True)

    with jax.named_scope("experts"):
        arrived_rows = arrived.reshape(seq_devices * share, width)
        done = run_expert(arrived_rows, lift_all, down_all)

    with jax.named_scope("combine"):
        returned = lax.all_to_all(
            done.reshape(seq_devices, share, width), "seq", split_axis=0, concat_axis=0, tiled=True
        )
        mixed_rows = jnp.dot(
            combiner,
            returned.reshape(seq_devices * share, width),
            preferred_element_type=jnp.float32,
        )
        term = mixed_rows.astype(jnp.bfloat16).reshape(exp_devices, own_rows, width)
        terms = lax.all_to_all(term, "exp", split_axis=0, concat_axis=0, tiled=True)
        expert_sum = jnp.sum(terms.astype(jnp.float32), axis=0)
        layer_out = (residual.astype(jnp.float32) + expert_sum).astype(jnp.bfloat16)
    return layer_out[None]


def solution(mesh):
    placed = (
        P("batch", "seq", "exp"),
        P("batch", "seq", "exp"),
        P("exp"),
        P("exp", None),
        P("batch", ("seq", "exp"), None),
        P(),
        P("batch", "seq", None),
        P("batch", "seq", None),
        P("seq", None, "exp"),
        P("seq", None, "exp"),
        P("seq", "exp", None),
    )
    return jax.shard_map(
        on_device,
        mesh=mesh,
        in_specs=placed,
        out_specs=P("batch", ("seq", "exp"), None),
        check_vma=False,
    )
```

time: 687 us -> 275 us (0.40)
  the two profiles are of different devices: /device:TPU:2 before, /device:TPU:32 now
where the time goes in v1:
time: 275 us; the launch traced here: 274 us
  blocking collectives  128 us (47%)
  waiting for transfers between devices  75.7 us (28%)
  starting transfers between devices  20.8 us (8%)
  between operations  13.7 us (5%)
  local copies, waits for them, and re-layouts  12.3 us (4%)
  Pallas kernels  12.3 us (4%)
  other arithmetic  7.18 us (3%)
  matrix products  4.18 us (2%)
    all_to_all x1, waiting for transfers between devices, on_device(): lax.all_to_all(copies, 'seq', split_axis=0, concat_axis=0, tiled=True)  53.9 us
    all_to_all x1, blocking collectives, on_device(): lax.all_to_all(done.reshape(seq_devices, share, width), 'seq', split_axis...  51.1 us
    all_to_all x1, blocking collectives, on_device(): lax.all_to_all(outgoing, 'seq', split_axis=0, concat_axis=0, tiled=True)  46.7 us
    all_to_all x1, waiting for transfers between devices, on_device(): lax.all_to_all(head_parts, 'exp', split_axis=0, concat_axis=0, tiled=True)  21 us
    all_to_all x1, starting transfers between devices, on_device(): lax.all_to_all(copies, 'seq', split_axis=0, concat_axis=0, tiled=True)  16.3 us
    all_to_all x1, blocking collectives, on_device(): terms = lax.all_to_all(term, 'exp', split_axis=0, concat_axis=0, tiled=True)  15.3 us
    all_gather x1, blocking collectives, on_device(): normed = lax.all_gather(normed_own, 'exp', axis=0, tiled=True)  15 us
    pallas_call x1, Pallas kernels, run_expert(): pl.pallas_call(expert_kernel, grid=(groups,), in_specs=[pl.BlockSpec((cou...  12.3 us
  transfers between devices with their start and end apart: 4, of which 2 were waited for; matrix products, arithmetic and copies ran while one was open for 7% of the time, Pallas kernels for 0%

profile of v1, /device:TPU:32, one launch (start us, length us, event | category | flops | bytes accessed | tf_op | source)
XLA Modules:
  0.0 274.3 jit_solution(4910202113324704477)
XLA Ops:
  6.5 0.7 all-gather.4.cloned.1.call-update
  7.3 2.0 copy.45
  9.3 2.5 copy.46
  11.9 4.4 %pad_maximum_fusion = bf16[2880,384]{1,0:T(8,128)(2,1)} fusion(bf16[2880,12]{1,0:T(8,128)(2,1)S(1)} %broadcast_in_dim.52, bf16[2880,180]{1,0:T(8,128)(2,1)} %bitcast.65, bf16[2880,180]{1,0:T(8,128)(2,1)S(1)} %bitcast.64), kind=kLoop, calls=%fused_computation.10 | loop fusion | flops 8847360 | bytes 4354560 | tf_op jit(solution)/shard_map/gather_weights/concatenate | solution.py:84
  16.4 1.3 broadcast_in_dim.24
  17.7 16.3 %all-to-all-start = ((bf16[32,128,128]{1,2,0:T(8,128)(2,1)}), bf16[32,128,128]{1,2,0:T(8,128)(2,1)S(1)}, u32[]{:S(2)}, u32[]{:S(2)}) async-start(bf16[32,128,128]{1,2,0:T(8,128)(2,1)} %broadcast_in_dim.24), calls=%async_computation | async-start | bytes 2097152 | tf_op jit(solution)/shard_map/gather_keys/all_to_all | solution.py:90
  34.2 0.3 iota_compare_fusion
  34.5 53.9 %all-to-all-done = bf16[32,128,128]{1,2,0:T(8,128)(2,1)S(1)} async-done(((bf16[32,128,128]{1,2,0:T(8,128)(2,1)}), bf16[32,128,128]{1,2,0:T(8,128)(2,1)S(1)}, u32[]{:S(2)}, u32[]{:S(2)}) %all-to-all-start) | async-done | bytes 1048608 | tf_op jit(solution)/shard_map/gather_keys/all_to_all | solution.py:90
  88.5 0.1 copy_bitcast_fusion
  88.6 1.3 fusion.34
  90.0 1.1 fusion
  91.2 1.4 fusion.12
  92.6 0.5 convolution_convert_fusion
  93.2 1.2 copy.43
  94.3 4.5 %all-to-all-start.1 = ((bf16[8,16,2880]{2,1,0:T(8,128)(2,1)}), bf16[8,16,2880]{2,1,0:T(8,128)(2,1)S(1)}, u32[]{:S(2)}, u32[]{:S(2)}) async-start(bf16[8,16,2880]{2,1,0:T(8,128)(2,1)} %bitcast.8), calls=%async_computation.1 | async-start | bytes 1507328 | tf_op jit(solution)/shard_map/project/all_to_all | solution.py:117
  98.9 0.1 fusion.24
  99.0 21.0 %all-to-all-done.1 = bf16[8,16,2880]{2,1,0:T(8,128)(2,1)S(1)} async-done(((bf16[8,16,2880]{2,1,0:T(8,128)(2,1)}), bf16[8,16,2880]{2,1,0:T(8,128)(2,1)S(1)}, u32[]{:S(2)}, u32[]{:S(2)}) %all-to-all-start.1) | async-done | bytes 737312 | tf_op jit(solution)/shard_map/project/all_to_all | solution.py:117
  120.0 0.1 convert_reduce_fusion.1
  120.1 0.2 fusion.20
  120.4 15.0 %all_gather.12 = bf16[128,2880]{1,0:T(8,128)(2,1)S(1)} all-gather(bf16[16,2880]{1,0:T(8,128)(2,1)S(1)} %fusion.22), channel_id=1, replica_groups=mesh['seq'=32,'exp'=8,'batch'=2] {'exp'}, dimensions={0}, use_global_device_ids=true | all-gather | bytes 829440 | tf_op jit(solution)/shard_map/norm/all_gather | solution.py:125
  135.4 0.4 convolution_convert_fusion.1
  135.8 0.4 copy.44
  136.2 46.7 %all_to_all.25 = bf16[32,3,2880]{2,1,0:T(4,128)(2,1)S(1)} all-to-all(bf16[32,3,2880]{2,1,0:T(4,128)(2,1)S(1)} %copy.44), channel_id=1, replica_groups=mesh['seq'=32,'exp'=8,'batch'=2] {'seq'}, dimensions={0} | all-to-all | bytes 1105920 | tf_op jit(solution)/shard_map/dispatch/all_to_all | solution.py:150
  182.9 0.5 reshape.103.rows_ref
  183.4 3.5 %copy-done.1 = bf16[8,180,2880]{2,1,0:T(8,128)(2,1)S(1)} copy-done((bf16[8,180,2880]{2,1,0:T(8,128)(2,1)S(1)}, bf16[8,180,2880]{2,1,0:T(8,128)(2,1)}, u32[]{:S(2)}) %copy-start.1) | copy-done | bytes 8294424
  186.9 12.3 %experts.1 = bf16[96,2880]{1,0:T(8,128)(2,1)S(1)} custom-call(bf16[96,2880]{1,0:T(8,128)(2,1)S(1)} %reshape.103.rows_ref, bf16[8,2880,384]{2,1,0:T(8,128)(2,1)} %bitcast.63, bf16[8,180,2880]{2,1,0:T(8,128)(2,1)S(1)} %copy-done.1), custom_call_target="tpu_custom_call" | custom-call | flops 2388787200 | bytes 25989120 | tf_op jit(solution)/shard_map/experts/pallas_call | solution.py:39
  199.2 0.3 reshape.104
  199.5 51.1 %all_to_all.26 = bf16[32,3,2880]{2,1,0:T(4,128)(2,1)S(1)} all-to-all(bf16[32,3,2880]{2,1,0:T(4,128)(2,1)S(1)} %reshape.104), channel_id=1, replica_groups=mesh['seq'=32,'exp'=8,'batch'=2] {'seq'}, dimensions={0} | all-to-all | bytes 1105920 | tf_op jit(solution)/shard_map/combine/all_to_all | solution.py:157
  250.6 0.4 fusion.5
  251.0 0.4 copy.48
  251.4 15.3 %all_to_all.27 = bf16[8,16,2880]{2,1,0:T(8,128)(2,1)S(1)} all-to-all(bf16[8,16,2880]{2,1,0:T(8,128)(2,1)S(1)} %bitcast.66), channel_id=1, replica_groups=mesh['seq'=32,'exp'=8,'batch'=2] {'exp'}, dimensions={0} | all-to-all | bytes 1474560 | tf_op jit(solution)/shard_map/combine/all_to_all | solution.py:166
  266.8 0.7 fusion.23
  (35 shorter events, 0.8 us)
Async XLA Ops:
  6.5 86.1 %copy-start = (bf16[256,2880]{0,1:T(8,128)(2,1)S(1)}, bf16[256,2880]{0,1:T(8,128)(2,1)}, u32[]{:S(2)}) copy-start(bf16[256,2880]{0,1:T(8,128)(2,1)} %param.14) | copy-start | bytes 4423684
  6.5 176.9 %all-gather.4.cloned.1.call-start = ((), (), s32[]{:S(2)}) async-start(), calls=%async_computation.5 | async-start | bytes 9750528 | tf_op jit(solution)/shard_map/gather_weights/all_gather | solution.py:86
  7.3 176.2 %all-gather.6.cloned.1.call-start = ((), (), s32[]{:S(2)}) async-start(), calls=%async_computation.6 | async-start | bytes 19906560 | tf_op jit(solution)/shard_map/gather_weights/all_gather | solution.py:85
  11.9 4.4 %copy-start.4 = (bf16[1,128,128]{2,1,0:T(8,128)(2,1)S(1)}, bf16[1,128,128]{2,1,0:T(8,128)(2,1)}, u32[]{:S(2)}) copy-start(bf16[1,128,128]{2,1,0:T(8,128)(2,1)} %param.12) | copy-start | bytes 98308
  16.3 17.7 %copy-start.3 = (bf16[1,128,256]{2,1,0:T(8,128)(2,1)S(1)}, bf16[1,128,256]{2,1,0:T(8,128)(2,1)}, u32[]{:S(2)}) copy-start(bf16[1,128,256]{2,1,0:T(8,128)(2,1)} %param.11) | copy-start | bytes 196612
  16.3 17.9 %copy-start.8 = (bf16[1,128,4]{1,2,0:T(4,128)(2,1)S(1)}, bf16[1,128,4]{1,2,0:T(4,128)(2,1)}, u32[]{:S(2)}) copy-start(bf16[1,128,4]{1,2,0:T(4,128)(2,1)} %param.18) | copy-start | bytes 3076
  17.7 70.8 %all-to-all-start = ((bf16[32,128,128]{1,2,0:T(8,128)(2,1)}), bf16[32,128,128]{1,2,0:T(8,128)(2,1)S(1)}, u32[]{:S(2)}, u32[]{:S(2)}) async-start(bf16[32,128,128]{1,2,0:T(8,128)(2,1)} %broadcast_in_dim.24), calls=%async_computation | async-start | bytes 2097152 | tf_op jit(solution)/shard_map/gather_keys/all_to_all | solution.py:90
  88.6 1.3 copy-start.7
  92.6 6.2 %copy-start.6 = (s32[1,128,4]{1,2,0:T(4,128)S(1)}, s32[1,128,4]{1,2,0:T(4,128)}, u32[]{:S(2)}) copy-start(s32[1,128,4]{1,2,0:T(4,128)} %param.17) | copy-start | bytes 6148
  92.6 27.5 %copy-start.2 = (bf16[1,16,2880]{2,1,0:T(8,128)(2,1)S(1)}, bf16[1,16,2880]{2,1,0:T(8,128)(2,1)}, u32[]{:S(2)}) copy-start(bf16[1,16,2880]{2,1,0:T(8,128)(2,1)} %param.15) | copy-start | bytes 276484
  92.6 27.7 %copy-start.5 = (f32[2880]{0:T(1024)S(1)}, f32[2880]{0:T(1024)}, u32[]{:S(2)}) copy-start(f32[2880]{0:T(1024)} %param.16) | copy-start | bytes 34564
  94.3 25.7 %all-to-all-start.1 = ((bf16[8,16,2880]{2,1,0:T(8,128)(2,1)}), bf16[8,16,2880]{2,1,0:T(8,128)(2,1)S(1)}, u32[]{:S(2)}, u32[]{:S(2)}) async-start(bf16[8,16,2880]{2,1,0:T(8,128)(2,1)} %bitcast.8), calls=%async_computation.1 | async-start | bytes 1507328 | tf_op jit(solution)/shard_map/project/all_to_all | solution.py:117
  183.4 3.5 %copy-start.1 = (bf16[8,180,2880]{2,1,0:T(8,128)(2,1)S(1)}, bf16[8,180,2880]{2,1,0:T(8,128)(2,1)}, u32[]{:S(2)}) copy-start(bf16[8,180,2880]{2,1,0:T(8,128)(2,1)} %all-gather.4.cloned.1.call-done.down_ref) | copy-start | bytes 24883204
Sparse Core Ops, SparseCore 0:
  9.5 62.6 all-gather.3
  74.4 107.8 all-gather.5

commit v2 on v1

v2 whole, which is shorter than its diff:
```python
import jax
import jax.numpy as jnp
from jax import lax
from jax.experimental import pallas as pl
from jax.experimental.pallas import tpu as pltpu
from jax.sharding import PartitionSpec as P

HEAD = 64
LIFT_ROWS = 368
CHUNK = 384
CAP = 24
RUN = 16


def pack_kernel(gate_ref, up_ref, down_ref, out_ref):
    units, width = gate_ref.shape
    spare = jnp.zeros((LIFT_ROWS - 2 * units, width), out_ref.dtype)
    out_ref[...] = jnp.concatenate([gate_ref[...], up_ref[...], spare, down_ref[...]], axis=0)


def pack_weights(gate_across, up_across, down):
    units, width = down.shape
    depth = LIFT_ROWS + units
    return pl.pallas_call(
        pack_kernel,
        out_shape=jax.ShapeDtypeStruct((depth, width), down.dtype),
        compiler_params=pltpu.CompilerParams(vmem_limit_bytes=24 * 1024 * 1024),
        cost_estimate=pl.CostEstimate(
            flops=0, bytes_accessed=4 * depth * width, transcendentals=0
        ),
    )(gate_across, up_across, down)


def expert_kernel(rows_ref, weight_ref, out_ref, total_ref):
    step = pl.program_id(0)
    units = weight_ref.shape[1] - LIFT_ROWS
    cut = LIFT_ROWS // 32 * 16
    rows = rows_ref[...]
    both = jnp.concatenate(
        [
            jnp.dot(weight_ref[0, :cut, :], rows, preferred_element_type=jnp.float32),
            jnp.dot(weight_ref[0, cut:LIFT_ROWS, :], rows, preferred_element_type=jnp.float32),
        ],
        axis=0,
    )
    gate = both[:units]
    lifted = both[units : 2 * units]
    hidden = gate * jax.nn.sigmoid(1.702 * gate) * (lifted + 1.0)

    @pl.when(step == 0)
    def _():
        total_ref[...] = jnp.zeros_like(total_ref)

    total_ref[...] += jnp.dot(
        hidden.T.astype(jnp.bfloat16),
        weight_ref[0, LIFT_ROWS:, :],
        preferred_element_type=jnp.float32,
    )

    @pl.when(step == pl.num_programs(0) - 1)
    def _():
        count, width = total_ref.shape
        chunks = out_ref.shape[0] // count
        part = 24
        side = part * chunks
        share = CAP // chunks
        row = lax.broadcasted_iota(jnp.int32, (side, side), 0)
        col = lax.broadcasted_iota(jnp.int32, (side, side), 1)
        block, rest = row // (chunks * share), row % (chunks * share)
        source = (rest // share) * part + block * share + rest % share
        turn = (source == col).astype(jnp.bfloat16)
        for first in range(0, count, part):
            pieces = []
            for chunk in range(chunks):
                low, high = chunk * CHUNK, min((chunk + 1) * CHUNK, width)
                piece = total_ref[first : first + part, low:high]
                if high - low < CHUNK:
                    fill = jnp.zeros((part, CHUNK - (high - low)), jnp.float32)
                    piece = jnp.concatenate([piece, fill], axis=1)
                pieces.append(piece)
            stacked = jnp.concatenate(pieces, axis=0).astype(jnp.bfloat16)
            out_ref[first * chunks : (first + part) * chunks, :] = jnp.dot(
                turn, stacked, preferred_element_type=jnp.float32
            ).astype(out_ref.dtype)


def run_expert(rows_across, weights):
    width, count = rows_across.shape
    groups, depth, _ = weights.shape
    chunks = -(-width // CHUNK)
    return pl.pallas_call(
        expert_kernel,
        grid=(groups,),
        in_specs=[
            pl.BlockSpec((width, count), lambda g: (0, 0)),
            pl.BlockSpec((1, depth, width), lambda g: (g, 0, 0)),
        ],
        out_specs=pl.BlockSpec((count * chunks, CHUNK), lambda g: (0, 0)),
        out_shape=jax.ShapeDtypeStruct((count * chunks, CHUNK), jnp.bfloat16),
        scratch_shapes=[pltpu.VMEM((count, width), jnp.float32)],
        compiler_params=pltpu.CompilerParams(vmem_limit_bytes=40 * 1024 * 1024),
        cost_estimate=pl.CostEstimate(
            flops=2 * count * width * depth * groups,
            bytes_accessed=groups * depth * width * 2,
            transcendentals=count * depth * groups // 3,
        ),
    )(rows_across, weights)


def on_device(
    queries,
    keys_values,
    sinks,
    out_weight,
    hidden_in,
    norm_gain,
    expert_ids,
    expert_gates,
    gate_weight,
    up_weight,
    down_weight,
):
    seq_devices = lax.axis_size("seq")
    exp_devices = lax.axis_size("exp")
    block_rows = queries.shape[1]
    heads = sinks.shape[0]
    width = out_weight.shape[1]
    own_rows = hidden_in.shape[1]
    units = gate_weight.shape[2]
    seq_rank = lax.axis_index("seq")
    exp_rank = lax.axis_index("exp")
    run_rows = RUN * block_rows
    runs = seq_devices // RUN

    with jax.named_scope("gather_weights"):
        weights = lax.all_gather(
            pack_weights(gate_weight[0].T, up_weight[0].T, down_weight[0]),
            "exp",
            axis=0,
            tiled=False,
        )

    with jax.named_scope("gather_keys"):
        run_groups = [[r * RUN + i for i in range(RUN)] for r in range(runs)]
        copies = jnp.broadcast_to(keys_values, (RUN,) + keys_values.shape[1:])
        near = lax.all_to_all(
            copies, "seq", split_axis=0, concat_axis=0, tiled=True, axis_index_groups=run_groups
        )
        near = near.reshape(run_rows, 2 * HEAD)
        far = lax.ppermute(near, "seq", [(i, i + RUN) for i in range(seq_devices - RUN)])

    with jax.named_scope("attend"):
        grid = queries[0].reshape(block_rows, heads, HEAD)
        query_pos = seq_rank * block_rows + jnp.arange(block_rows, dtype=jnp.int32)
        first_near = (seq_rank // RUN) * run_rows
        offsets = jnp.arange(run_rows, dtype=jnp.int32)

        def score(keys, key_pos, keep):
            raw = (
                jnp.einsum("igd,jd->gij", grid, keys, preferred_element_type=jnp.float32) * 0.125
            )
            return jnp.where((key_pos[None, :] <= query_pos[:, None]) & keep, raw, -1e30)

        near_scores = score(near[:, :HEAD], first_near + offsets, True)
        far_scores = score(far[:, :HEAD], first_near - run_rows + offsets, seq_rank >= RUN)
        largest = jnp.maximum(
            jnp.maximum(jnp.max(near_scores, axis=-1), jnp.max(far_scores, axis=-1)),
            sinks[:, None],
        )
        near_top = jnp.exp(near_scores - largest[..., None])
        far_top = jnp.exp(far_scores - largest[..., None])
        totals = (
            jnp.sum(near_top, axis=-1)
            + jnp.sum(far_top, axis=-1)
            + jnp.exp(sinks[:, None] - largest)
        )
        weighted = jnp.einsum(
            "gij,jd->gid",
            near_top.astype(jnp.bfloat16),
            near[:, HEAD:],
            preferred_element_type=jnp.float32,
        ) + jnp.einsum(
            "gij,jd->gid",
            far_top.astype(jnp.bfloat16),
            far[:, HEAD:],
            preferred_element_type=jnp.float32,
        )
        mixed = (weighted / totals[..., None]).astype(jnp.bfloat16)
        heads_out = mixed.transpose(1, 0, 2).reshape(block_rows, heads * HEAD)

    with jax.named_scope("project"):
        head_term = jnp.dot(heads_out, out_weight, preferred_element_type=jnp.float32)
        head_parts = head_term.astype(jnp.bfloat16).reshape(exp_devices, own_rows, width)
        own_parts = lax.all_to_all(head_parts, "exp", split_axis=0, concat_axis=0, tiled=True)
        attention = jnp.sum(own_parts.astype(jnp.float32), axis=0)
        residual = (hidden_in[0].astype(jnp.float32) + attention).astype(jnp.bfloat16)

    with jax.named_scope("norm"):
        stream = residual.astype(jnp.float32)
        mean_square = jnp.mean(stream * stream, axis=-1, keepdims=True)
        normed_own = (stream * lax.rsqrt(mean_square + 1e-05) * norm_gain).astype(jnp.bfloat16)
        normed = lax.all_gather(normed_own, "exp", axis=0, tiled=True)

    with jax.named_scope("route"):
        chosen = expert_ids[0]
        share = CAP // exp_devices
        hits = (chosen[:, :, None] == jnp.arange(seq_devices, dtype=jnp.int32)).astype(jnp.float32)
        token_hits = jnp.sum(hits, axis=1)
        earlier = (
            jnp.arange(block_rows)[:, None] > jnp.arange(block_rows)[None, :]
        ).astype(jnp.float32)
        slots = jnp.dot(earlier, token_hits)
        named = token_hits[:, :, None] > 0
        wanted = (exp_rank * share + jnp.arange(share, dtype=jnp.int32)).astype(jnp.float32)
        picks = named & (slots[:, :, None] == wanted)
        selector = picks.astype(jnp.bfloat16)
        factor = jnp.einsum("tke,tk->te", hits, expert_gates[0].astype(jnp.float32))
        combiner = jnp.where(picks, factor[:, :, None], 0.0).astype(jnp.bfloat16)
        chunks = -(-width // CHUNK)
        by_owner = combiner.reshape(exp_devices, 1, own_rows, seq_devices, 1, share)
        same = jnp.eye(chunks, dtype=jnp.bfloat16).reshape(1, chunks, 1, 1, chunks, 1)
        combiner = (by_owner * same).reshape(
            exp_devices * chunks * own_rows, seq_devices * chunks * share
        )

    with jax.named_scope("dispatch"):
        outgoing = jnp.einsum(
            "tec,td->ecd", selector, normed, preferred_element_type=jnp.float32
        ).astype(jnp.bfloat16)
        arrived = lax.all_to_all(outgoing, "seq", split_axis=0, concat_axis=0, tiled=True)

    with jax.named_scope("experts"):
        rows_across = arrived.reshape(seq_devices * share, width).T
        done = run_expert(rows_across, weights)

    with jax.named_scope("combine"):
        returned = lax.all_to_all(
            done.reshape(seq_devices, chunks * share, CHUNK),
            "seq",
            split_axis=0,
            concat_axis=0,
            tiled=True,
        )
        mixed_rows = jnp.dot(
            combiner,
            returned.reshape(seq_devices * chunks * share, CHUNK),
            preferred_element_type=jnp.float32,
        )
        term = mixed_rows.astype(jnp.bfloat16).reshape(exp_devices, chunks * own_rows, CHUNK)
        terms = lax.all_to_all(term, "exp", split_axis=0, concat_axis=0, tiled=True)
        expert_sum = jnp.sum(terms.astype(jnp.float32), axis=0)
        expert_sum = expert_sum.reshape(chunks, own_rows, CHUNK).transpose(1, 0, 2)
        expert_sum = expert_sum.reshape(own_rows, chunks * CHUNK)[:, :width]
        layer_out = (residual.astype(jnp.float32) + expert_sum).astype(jnp.bfloat16)
    return layer_out[None]


def solution(mesh):
    placed = (
        P("batch", "seq", "exp"),
        P("batch", "seq", "exp"),
        P("exp"),
        P("exp", None),
        P("batch", ("seq", "exp"), None),
        P(),
        P("batch", "seq", None),
        P("batch", "seq", None),
        P("seq", None, "exp"),
        P("seq", None, "exp"),
        P("seq", "exp", None),
    )
    return jax.shard_map(
        on_device,
        mesh=mesh,
        in_specs=placed,
        out_specs=P("batch", ("seq", "exp"), None),
        check_vma=False,
    )
```

time: 275 us -> 252 us (0.916)
  blocking collectives: 128 us -> 86.7 us
  local copies, waits for them, and re-layouts: 12.3 us -> 32 us
  waiting for transfers between devices: 75.7 us -> 60.1 us
  starting transfers between devices: 20.8 us -> 27.7 us
  Pallas kernels: 12.3 us -> 15.3 us
    all_to_all x1 -> x0, blocking collectives: 51.1 us -> none  [on_device(): lax.all_to_all(done.reshape(seq_devices, share, width), 'seq', split_axis...]
    mul x0 -> x1, local copies, waits for them, and re-layouts: none -> 22.1 us  [on_device(): by_owner * same]
    all_to_all x1 -> x2, waiting for transfers between devices: 53.9 us -> 32.7 us  [the longest x1 26.7 us: on_device(): lax.all_to_all(copies, 'seq', split_axis=0, concat_axis=0, tiled=True, ax...]
    all_to_all x1, blocking collectives: 46.7 us -> 55.9 us  [on_device(): lax.all_to_all(outgoing, 'seq', split_axis=0, concat_axis=0, tiled=True)]
    ppermute x0 -> x1, waiting for transfers between devices: none -> 6.33 us  [on_device(): lax.ppermute(near, 'seq', [(i, i + RUN) for i in range(seq_devices - RUN)])]
    mul x0 -> x1, other arithmetic: none -> 5.43 us  [on_device(): by_owner * same]
    concatenate x1 -> x0, other arithmetic: 4.4 us -> none  [on_device(): jnp.concatenate([gate_weight[0], zeros, up_weight[0], zeros], axis=1)]
    all_to_all x1 -> x2, starting transfers between devices: 16.3 us -> 19.8 us  [the longest x1 15.2 us: on_device(): lax.all_to_all(copies, 'seq', split_axis=0, concat_axis=0, tiled=True, ax...]
  transfers between devices with their start and end apart: 4 -> 5, of which waited for: 2 -> 4; matrix products, arithmetic and copies ran while one was open for 7% -> 16% of each run, Pallas kernels for 0% -> 0%
where the time goes in v2:
time: 252 us; the launch traced here: 251 us
  blocking collectives  86.7 us (34%)
  waiting for transfers between devices  60.1 us (24%)
  local copies, waits for them, and re-layouts  32 us (13%)
  starting transfers between devices  27.7 us (11%)
  Pallas kernels  15.3 us (6%)
  between operations  13.7 us (5%)
  other arithmetic  9.36 us (4%)
  matrix products  6.26 us (2%)
    all_to_all x1, blocking collectives, on_device(): lax.all_to_all(outgoing, 'seq', split_axis=0, concat_axis=0, tiled=True)  55.9 us
    all_to_all x1, waiting for transfers between devices, on_device(): lax.all_to_all(copies, 'seq', split_axis=0, concat_axis=0, tiled=True, ax...  26.7 us
    mul x1, local copies, waits for them, and re-layouts, on_device(): by_owner * same  22.1 us
    all_to_all x1, waiting for transfers between devices, on_device(): lax.all_to_all(head_parts, 'exp', split_axis=0, concat_axis=0, tiled=True)  21 us
    all_to_all x1, blocking collectives, on_device(): terms = lax.all_to_all(term, 'exp', split_axis=0, concat_axis=0, tiled=True)  15.8 us
    all_to_all x1, starting transfers between devices, on_device(): lax.all_to_all(copies, 'seq', split_axis=0, concat_axis=0, tiled=True, ax...  15.2 us
    all_gather x1, blocking collectives, on_device(): normed = lax.all_gather(normed_own, 'exp', axis=0, tiled=True)  15 us
    pallas_call x1, Pallas kernels, run_expert(): pl.pallas_call(expert_kernel, grid=(groups,), in_specs=[pl.BlockSpec((wid...  15 us
  transfers between devices with their start and end apart: 5, of which 4 were waited for; matrix products, arithmetic and copies ran while one was open for 16% of the time, Pallas kernels for 0%

profile of v2, /device:TPU:32, one launch (start us, length us, event | category | flops | bytes accessed | tf_op | source)
XLA Modules:
  0.0 251.1 jit_solution(9064959624799501171)
XLA Ops:
  6.5 1.3 copy-done.3
  7.9 1.2 copy-done.4
  9.1 1.2 copy-done.5
  10.7 1.7 copy-done.2
  12.5 0.9 broadcast_in_dim.56
  13.4 15.2 %all-to-all-start = ((bf16[16,128,128]{1,2,0:T(8,128)(2,1)}), bf16[16,128,128]{1,2,0:T(8,128)(2,1)S(1)}, u32[]{:S(2)}, u32[]{:S(2)}) async-start(bf16[16,128,128]{1,2,0:T(8,128)(2,1)} %broadcast_in_dim.56), calls=%async_computation | async-start | bytes 1048576 | tf_op jit(solution)/shard_map/gather_keys/all_to_all | solution.py:146
  28.8 1.3 compare_and_fusion
  30.1 26.7 %all-to-all-done = bf16[16,128,128]{1,2,0:T(8,128)(2,1)S(1)} async-done(((bf16[16,128,128]{1,2,0:T(8,128)(2,1)}), bf16[16,128,128]{1,2,0:T(8,128)(2,1)S(1)}, u32[]{:S(2)}, u32[]{:S(2)}) %all-to-all-start) | async-done | bytes 524320 | tf_op jit(solution)/shard_map/gather_keys/all_to_all | solution.py:146
  56.9 3.4 %collective-permute-start = (bf16[2048,128]{0,1:T(8,128)(2,1)S(1)}, bf16[2048,128]{0,1:T(8,128)(2,1)S(1)}, u32[]{:S(2)}, u32[]{:S(2)}) collective-permute-start(bf16[2048,128]{0,1:T(8,128)(2,1)S(1)} %copy_bitcast_fusion), channel_id=1, source_target_pairs={{0,256},{16,272},{32,288},{48,304},{64,320},{80,336},{96,352},{112... | collective-permute-start | bytes 1572872 | tf_op jit(solution)/shard_map/gather_keys/ppermute | solution.py:150
  60.4 0.8 fusion.37
  61.1 6.3 %collective-permute-done = bf16[2048,128]{0,1:T(8,128)(2,1)S(1)} collective-permute-done((bf16[2048,128]{0,1:T(8,128)(2,1)S(1)}, bf16[2048,128]{0,1:T(8,128)(2,1)S(1)}, u32[]{:S(2)}, u32[]{:S(2)}) %collective-permute-start) | collective-permute-done | bytes 524320 | tf_op jit(solution)/shard_map/gather_keys/ppermute | solution.py:150
  67.5 0.7 fusion.38
  68.3 1.1 fusion.2
  69.5 0.8 fusion.6
  70.3 0.8 fusion.19
  71.1 0.5 convolution_convert_fusion
  71.6 1.2 copy.68
  72.8 4.5 %all-to-all-start.1 = ((bf16[8,16,2880]{2,1,0:T(8,128)(2,1)}), bf16[8,16,2880]{2,1,0:T(8,128)(2,1)S(1)}, u32[]{:S(2)}, u32[]{:S(2)}) async-start(bf16[8,16,2880]{2,1,0:T(8,128)(2,1)} %bitcast.12), calls=%async_computation.1 | async-start | bytes 1507328 | tf_op jit(solution)/shard_map/project/all_to_all | solution.py:194
  77.5 21.0 %all-to-all-done.1 = bf16[8,16,2880]{2,1,0:T(8,128)(2,1)S(1)} async-done(((bf16[8,16,2880]{2,1,0:T(8,128)(2,1)}), bf16[8,16,2880]{2,1,0:T(8,128)(2,1)S(1)}, u32[]{:S(2)}, u32[]{:S(2)}) %all-to-all-start.1) | async-done | bytes 737312 | tf_op jit(solution)/shard_map/project/all_to_all | solution.py:194
  98.9 15.0 %all_gather.9 = bf16[128,2880]{1,0:T(8,128)(2,1)S(1)} all-gather(bf16[16,2880]{1,0:T(8,128)(2,1)S(1)} %fusion.25), channel_id=1, replica_groups=mesh['seq'=32,'exp'=8,'batch'=2] {'exp'}, dimensions={0}, use_global_device_ids=true | all-gather | bytes 829440 | tf_op jit(solution)/shard_map/norm/all_gather | solution.py:202
  113.9 0.4 convolution_convert_fusion.1
  114.3 0.4 copy.74
  114.7 55.9 %all_to_all.25 = bf16[32,3,2880]{2,1,0:T(4,128)(2,1)S(1)} all-to-all(bf16[32,3,2880]{2,1,0:T(4,128)(2,1)S(1)} %copy.74), channel_id=1, replica_groups=mesh['seq'=32,'exp'=8,'batch'=2] {'seq'}, dimensions={0} | all-to-all | bytes 1105920 | tf_op jit(solution)/shard_map/dispatch/all_to_all | solution.py:230
  170.5 0.5 reshape.166
  171.4 15.0 %experts.1 = bf16[768,384]{1,0:T(8,128)(2,1)} custom-call(bf16[2880,96]{1,0:T(8,128)(2,1)S(1)} %bitcast.81, bf16[8,548,2880]{2,1,0:T(8,128)(2,1)} %all-gather.4.cloned.1.call-done.weight_ref), custom_call_target="tpu_custom_call" | custom-call | flops 2424176640 | bytes 25251840 | tf_op jit(solution)/shard_map/experts/pallas_call | solution.py:91
  186.4 4.6 %all-to-all-start.3 = ((bf16[32,24,384]{2,1,0:T(8,128)(2,1)}), bf16[32,24,384]{2,1,0:T(8,128)(2,1)}, u32[]{:S(2)}, u32[]{:S(2)}) async-start(bf16[32,24,384]{2,1,0:T(8,128)(2,1)} %bitcast.26), calls=%async_computation.3 | async-start | bytes 1179648 | tf_op jit(solution)/shard_map/combine/all_to_all | solution.py:237
  191.9 5.4 %broadcast_multiply_fusion = bf16[8,8,16,32,8,3]{2,1,0,5,4,3:T(8,128)(2,1)} fusion(bf16[8,8]{0,1:T(8,128)(2,1)S(1)} %fusion.35, bf16[8,16,32,3]{1,0,3,2:T(8,128)(2,1)S(1)} %select_convert_fusion), kind=kLoop, calls=%fused_computation | loop fusion | flops 786432 | bytes 1597568 | tf_op jit(solution)/shard_map/route/mul | solution.py:222
  197.3 22.1 %mul.73 = bf16[1024,768]{0,1:T(8,128)(2,1)S(1)} reshape(bf16[8,8,16,32,8,3]{2,1,0,5,4,3:T(8,128)(2,1)} %broadcast_multiply_fusion) | data formatting | bytes 3145728 | tf_op jit(solution)/shard_map/route/mul | solution.py:222
  219.4 6.0 %all-to-all-done.3 = bf16[32,24,384]{2,1,0:T(8,128)(2,1)} async-done(((bf16[32,24,384]{2,1,0:T(8,128)(2,1)}), bf16[32,24,384]{2,1,0:T(8,128)(2,1)}, u32[]{:S(2)}, u32[]{:S(2)}) %all-to-all-start.3) | async-done | bytes 589856 | tf_op jit(solution)/shard_map/combine/all_to_all | solution.py:237
  225.5 2.2 convolution_convert_fusion.2
  227.7 15.8 %all_to_all.26 = bf16[8,128,384]{2,1,0:T(8,128)(2,1)S(1)} all-to-all(bf16[8,128,384]{2,1,0:T(8,128)(2,1)S(1)} %bitcast.85), channel_id=1, replica_groups=mesh['seq'=32,'exp'=8,'batch'=2] {'exp'}, dimensions={0} | all-to-all | bytes 1572864 | tf_op jit(solution)/shard_map/combine/all_to_all | solution.py:250
  243.6 0.7 fusion.28
  (53 shorter events, 2.7 us)
Async XLA Ops:
  6.5 64.5 %copy-start = (bf16[256,2880]{0,1:T(8,128)(2,1)S(1)}, bf16[256,2880]{0,1:T(8,128)(2,1)}, u32[]{:S(2)}) copy-start(bf16[256,2880]{0,1:T(8,128)(2,1)} %param.14) | copy-start | bytes 4423684
  6.5 164.9 %all-gather.4.cloned.1.call-start = ((), (), s32[]{:S(2)}) async-start(), calls=%async_computation.5 | async-start | bytes 29251584 | tf_op jit(solution)/shard_map/gather_weights/all_gather | solution.py:136
  6.5 1.4 copy-start.3
  7.9 1.2 copy-start.4
  9.1 1.2 copy-start.5
  10.4 2.0 copy-start.8
  10.4 18.2 %copy-start.7 = (bf16[1,128,256]{2,1,0:T(8,128)(2,1)S(1)}, bf16[1,128,256]{2,1,0:T(8,128)(2,1)}, u32[]{:S(2)}) copy-start(bf16[1,128,256]{2,1,0:T(8,128)(2,1)} %param.11) | copy-start | bytes 196612
  10.6 1.7 copy-start.2
  12.3 48.1 %copy-start.12 = (bf16[1,128,4]{1,2,0:T(4,128)(2,1)S(1)}, bf16[1,128,4]{1,2,0:T(4,128)(2,1)}, u32[]{:S(2)}) copy-start(bf16[1,128,4]{1,2,0:T(4,128)(2,1)} %param.18) | copy-start | bytes 3076
  13.4 43.4 %all-to-all-start = ((bf16[16,128,128]{1,2,0:T(8,128)(2,1)}), bf16[16,128,128]{1,2,0:T(8,128)(2,1)S(1)}, u32[]{:S(2)}, u32[]{:S(2)}) async-start(bf16[16,128,128]{1,2,0:T(8,128)(2,1)} %broadcast_in_dim.56), calls=%async_computation | async-start | bytes 1048576 | tf_op jit(solution)/shard_map/gather_keys/all_to_all | solution.py:146
  56.9 10.6 %collective-permute-start = (bf16[2048,128]{0,1:T(8,128)(2,1)S(1)}, bf16[2048,128]{0,1:T(8,128)(2,1)S(1)}, u32[]{:S(2)}, u32[]{:S(2)}) collective-permute-start(bf16[2048,128]{0,1:T(8,128)(2,1)S(1)} %copy_bitcast_fusion), channel_id=1, source_target_pairs={{0,256},{16,272},{32,288},{48,304},{64,320},{80,336},{96,352},{112... | collective-permute-start | bytes 1572872 | tf_op jit(solution)/shard_map/gather_keys/ppermute | solution.py:150
  60.4 7.8 %copy-start.11 = (f32[4]{0:T(128)S(1)}, f32[4]{0:T(128)}, u32[]{:S(2)}) copy-start(f32[4]{0:T(128)} %param.13) | copy-start | bytes 52
  70.3 7.0 %copy-start.10 = (s32[1,128,4]{1,2,0:T(4,128)S(1)}, s32[1,128,4]{1,2,0:T(4,128)}, u32[]{:S(2)}) copy-start(s32[1,128,4]{1,2,0:T(4,128)} %param.17) | copy-start | bytes 6148
  71.0 27.6 %copy-start.6 = (bf16[1,16,2880]{2,1,0:T(8,128)(2,1)S(1)}, bf16[1,16,2880]{2,1,0:T(8,128)(2,1)}, u32[]{:S(2)}) copy-start(bf16[1,16,2880]{2,1,0:T(8,128)(2,1)} %param.15) | copy-start | bytes 276484
  71.0 27.7 %copy-start.9 = (f32[2880]{0:T(1024)S(1)}, f32[2880]{0:T(1024)}, u32[]{:S(2)}) copy-start(f32[2880]{0:T(1024)} %param.16) | copy-start | bytes 34564
  72.8 25.7 %all-to-all-start.1 = ((bf16[8,16,2880]{2,1,0:T(8,128)(2,1)}), bf16[8,16,2880]{2,1,0:T(8,128)(2,1)S(1)}, u32[]{:S(2)}, u32[]{:S(2)}) async-start(bf16[8,16,2880]{2,1,0:T(8,128)(2,1)} %bitcast.12), calls=%async_computation.1 | async-start | bytes 1507328 | tf_op jit(solution)/shard_map/project/all_to_all | solution.py:194
  186.4 39.0 %all-to-all-start.3 = ((bf16[32,24,384]{2,1,0:T(8,128)(2,1)}), bf16[32,24,384]{2,1,0:T(8,128)(2,1)}, u32[]{:S(2)}, u32[]{:S(2)}) async-start(bf16[32,24,384]{2,1,0:T(8,128)(2,1)} %bitcast.26), calls=%async_computation.3 | async-start | bytes 1179648 | tf_op jit(solution)/shard_map/combine/all_to_all | solution.py:237
  225.5 18.8 %copy-start.1 = (bf16[256,2880]{0,1:T(8,128)(2,1)S(1)}, bf16[256,2880]{0,1:T(8,128)(2,1)}, u32[]{:S(2)}) copy-start(bf16[256,2880]{0,1:T(8,128)(2,1)} %param.14) | copy-start | bytes 4423684
Sparse Core Ops, SparseCore 0:
  12.5 146.6 all-gather.3

commit v3 on v2

v3 whole, which is shorter than its diff:
```python
import jax
import jax.numpy as jnp
from jax import lax
from jax.experimental import pallas as pl
from jax.experimental.pallas import tpu as pltpu
from jax.sharding import PartitionSpec as P

HEAD = 64
LIFT_ROWS = 368
CHUNK = 384
CAP = 24
GROUP = 24
CORES = 2
RUN = 16


def pack_kernel(gate_ref, up_ref, down_ref, out_ref):
    units, width = gate_ref.shape
    spare = jnp.zeros((LIFT_ROWS - 2 * units, width), out_ref.dtype)
    out_ref[...] = jnp.concatenate([gate_ref[...], up_ref[...], spare, down_ref[...]], axis=0)


def pack_weights(gate_across, up_across, down):
    units, width = down.shape
    depth = LIFT_ROWS + units
    return pl.pallas_call(
        pack_kernel,
        out_shape=jax.ShapeDtypeStruct((depth, width), down.dtype),
        compiler_params=pltpu.CompilerParams(vmem_limit_bytes=56 * 1024 * 1024),
        cost_estimate=pl.CostEstimate(
            flops=0, bytes_accessed=4 * depth * width, transcendentals=0
        ),
    )(gate_across, up_across, down)


def chunk_turn(chunks, back):
    side = GROUP * chunks
    share = CAP // chunks
    row = lax.broadcasted_iota(jnp.int32, (side, side), 1 if back else 0)
    col = lax.broadcasted_iota(jnp.int32, (side, side), 0 if back else 1)
    block, rest = row // (chunks * share), row % (chunks * share)
    source = (rest // share) * GROUP + block * share + rest % share
    return (source == col).astype(jnp.bfloat16)


def store_chunks(rows_ref, out_ref):
    count, width = rows_ref.shape
    chunks = out_ref.shape[0] // count
    turn = chunk_turn(chunks, False)
    for first in range(0, count, GROUP):
        pieces = []
        for chunk in range(chunks):
            low, high = chunk * CHUNK, min((chunk + 1) * CHUNK, width)
            piece = rows_ref[first : first + GROUP, low:high]
            if high - low < CHUNK:
                fill = jnp.zeros((GROUP, CHUNK - (high - low)), piece.dtype)
                piece = jnp.concatenate([piece, fill], axis=1)
            pieces.append(piece)
        stacked = jnp.concatenate(pieces, axis=0).astype(jnp.bfloat16)
        out_ref[first * chunks : (first + GROUP) * chunks, :] = jnp.dot(
            turn, stacked, preferred_element_type=jnp.float32
        ).astype(out_ref.dtype)


def load_chunks(chunks_ref, count):
    chunks = chunks_ref.shape[0] // count
    turn = chunk_turn(chunks, True)
    rows = []
    for first in range(0, count, GROUP):
        stacked = jnp.dot(
            turn,
            chunks_ref[first * chunks : (first + GROUP) * chunks, :],
            preferred_element_type=jnp.float32,
        )
        rows.append(
            jnp.concatenate([stacked[i * GROUP : (i + 1) * GROUP] for i in range(chunks)], axis=1)
        )
    return jnp.concatenate(rows, axis=0)


def combine_kernel(combiner_ref, chunks_ref, out_ref):
    width = out_ref.shape[1]
    rows = load_chunks(chunks_ref, combiner_ref.shape[1])[:, :width].astype(jnp.bfloat16)
    out_ref[...] = jnp.dot(
        combiner_ref[...], rows, preferred_element_type=jnp.float32
    ).astype(out_ref.dtype)


def run_combine(combiner, chunk_rows, width):
    tokens, count = combiner.shape
    return pl.pallas_call(
        combine_kernel,
        out_shape=jax.ShapeDtypeStruct((tokens, width), jnp.bfloat16),
        compiler_params=pltpu.CompilerParams(vmem_limit_bytes=24 * 1024 * 1024),
        cost_estimate=pl.CostEstimate(
            flops=2 * tokens * count * width, bytes_accessed=4 * tokens * width, transcendentals=0
        ),
    )(combiner, chunk_rows)


def select_kernel(selector_ref, normed_ref, out_ref, rows_ref):
    rows_ref[...] = jnp.dot(
        selector_ref[...], normed_ref[...], preferred_element_type=jnp.float32
    )
    store_chunks(rows_ref, out_ref)


def run_select(selector, normed):
    count, depth = selector.shape
    width = normed.shape[1]
    chunks = -(-width // CHUNK)
    return pl.pallas_call(
        select_kernel,
        out_shape=jax.ShapeDtypeStruct((count * chunks, CHUNK), jnp.bfloat16),
        scratch_shapes=[pltpu.VMEM((count, width), jnp.float32)],
        compiler_params=pltpu.CompilerParams(vmem_limit_bytes=24 * 1024 * 1024),
        cost_estimate=pl.CostEstimate(
            flops=4 * count * depth * width, bytes_accessed=4 * count * width, transcendentals=0
        ),
    )(selector, normed)


def expert_kernel(chunks_ref, weight_ref, out_ref, total_ref, across_ref):
    step = pl.program_id(0)
    units = weight_ref.shape[1] - LIFT_ROWS
    cut = LIFT_ROWS // 32 * 16
    count, width = total_ref.shape
    chunks = chunks_ref.shape[0] // count

    @pl.when(step == 0)
    def _():
        total_ref[...] = jnp.zeros_like(total_ref)
        across = load_chunks(chunks_ref, count).T
        across_ref[...] = across[:width].astype(across_ref.dtype)

    rows_across = across_ref[...]
    both = jnp.concatenate(
        [
            jnp.dot(weight_ref[0, :cut, :], rows_across, preferred_element_type=jnp.float32),
            jnp.dot(
                weight_ref[0, cut:LIFT_ROWS, :], rows_across, preferred_element_type=jnp.float32
            ),
        ],
        axis=0,
    )
    gate = both[:units]
    lifted = both[units : 2 * units]
    hidden = gate * jax.nn.sigmoid(1.702 * gate) * (lifted + 1.0)
    total_ref[...] += jnp.dot(
        hidden.T.astype(jnp.bfloat16),
        weight_ref[0, LIFT_ROWS:, :],
        preferred_element_type=jnp.float32,
    )

    @pl.when(step == pl.num_programs(0) - 1)
    def _():
        store_chunks(total_ref, out_ref)


def run_expert(chunk_rows, weights):
    groups, depth, width = weights.shape
    chunks = -(-width // CHUNK)
    count = chunk_rows.shape[0] // chunks
    return pl.pallas_call(
        expert_kernel,
        grid=(groups,),
        in_specs=[
            pl.BlockSpec((count * chunks, CHUNK), lambda g: (0, 0)),
            pl.BlockSpec((1, depth, width), lambda g: (g, 0, 0)),
        ],
        out_specs=pl.BlockSpec((count * chunks, CHUNK), lambda g: (0, 0)),
        out_shape=jax.ShapeDtypeStruct((count * chunks, CHUNK), jnp.bfloat16),
        scratch_shapes=[
            pltpu.VMEM((count, width), jnp.float32),
            pltpu.VMEM((width, count), jnp.bfloat16),
        ],
        compiler_params=pltpu.CompilerParams(vmem_limit_bytes=40 * 1024 * 1024),
        cost_estimate=pl.CostEstimate(
            flops=2 * count * width * depth * groups,
            bytes_accessed=groups * depth * width * 2,
            transcendentals=count * depth * groups // 3,
        ),
    )(chunk_rows, weights)


def on_device(
    queries,
    keys_values,
    sinks,
    out_weight,
    hidden_in,
    norm_gain,
    expert_ids,
    expert_gates,
    gate_weight,
    up_weight,
    down_weight,
):
    seq_devices = lax.axis_size("seq")
    exp_devices = lax.axis_size("exp")
    block_rows = queries.shape[1]
    heads = sinks.shape[0]
    width = out_weight.shape[1]
    own_rows = hidden_in.shape[1]
    units = gate_weight.shape[2]
    seq_rank = lax.axis_index("seq")
    exp_rank = lax.axis_index("exp")
    run_rows = RUN * block_rows
    runs = seq_devices // RUN

    with jax.named_scope("gather_weights"):
        weights = lax.all_gather(
            pack_weights(gate_weight[0].T, up_weight[0].T, down_weight[0]),
            "exp",
            axis=0,
            tiled=False,
        )

    with jax.named_scope("gather_keys"):
        run_groups = [[r * RUN + i for i in range(RUN)] for r in range(runs)]
        copies = jnp.broadcast_to(keys_values, (RUN,) + keys_values.shape[1:])
        near = lax.all_to_all(
            copies, "seq", split_axis=0, concat_axis=0, tiled=True, axis_index_groups=run_groups
        )
        near = near.reshape(run_rows, 2 * HEAD)
        far = lax.ppermute(near, "seq", [(i, i + RUN) for i in range(seq_devices - RUN)])

    with jax.named_scope("attend"):
        grid = queries[0].reshape(block_rows, heads, HEAD)
        query_pos = seq_rank * block_rows + jnp.arange(block_rows, dtype=jnp.int32)
        first_near = (seq_rank // RUN) * run_rows
        offsets = jnp.arange(run_rows, dtype=jnp.int32)

        def score(keys, key_pos, keep):
            raw = (
                jnp.einsum("igd,jd->gij", grid, keys, preferred_element_type=jnp.float32) * 0.125
            )
            return jnp.where((key_pos[None, :] <= query_pos[:, None]) & keep, raw, -1e30)

        def part(rows, key_pos, keep):
            scores = score(rows[:, :HEAD], key_pos, keep)
            top = jnp.max(scores, axis=-1)
            numerators = jnp.exp(scores - top[..., None])
            weighted = jnp.einsum(
                "gij,jd->gid",
                numerators.astype(jnp.bfloat16),
                rows[:, HEAD:],
                preferred_element_type=jnp.float32,
            )
            return top, jnp.sum(numerators, axis=-1), weighted

        near_top, near_sum, near_mix = part(near, first_near + offsets, True)
        far_top, far_sum, far_mix = part(far, first_near - run_rows + offsets, seq_rank >= RUN)
        largest = jnp.maximum(jnp.maximum(near_top, far_top), sinks[:, None])
        near_scale = jnp.exp(near_top - largest)
        far_scale = jnp.exp(far_top - largest)
        totals = near_sum * near_scale + far_sum * far_scale + jnp.exp(sinks[:, None] - largest)
        weighted = near_mix * near_scale[..., None] + far_mix * far_scale[..., None]
        mixed = (weighted / totals[..., None]).astype(jnp.bfloat16)
        heads_out = mixed.transpose(1, 0, 2).reshape(block_rows, heads * HEAD)

    with jax.named_scope("project"):
        head_term = jnp.dot(heads_out, out_weight, preferred_element_type=jnp.float32)
        chips = exp_devices // CORES
        core = exp_rank % CORES
        head_parts = head_term.reshape(chips, CORES, own_rows, width)
        given = lax.dynamic_index_in_dim(head_parts, 1 - core, 1, keepdims=False)
        kept = lax.dynamic_index_in_dim(head_parts, core, 1, keepdims=False)
        taken = lax.ppermute(
            given.astype(jnp.bfloat16), "exp", [(i, i ^ 1) for i in range(exp_devices)]
        )
        pair = (kept + taken.astype(jnp.float32)).astype(jnp.bfloat16)
        columns = [[CORES * i + c for i in range(chips)] for c in range(CORES)]
        own_parts = lax.all_to_all(
            pair, "exp", split_axis=0, concat_axis=0, tiled=True, axis_index_groups=columns
        )
        attention = jnp.sum(own_parts.astype(jnp.float32), axis=0)
        residual = (hidden_in[0].astype(jnp.float32) + attention).astype(jnp.bfloat16)

    with jax.named_scope("norm"):
        stream = residual.astype(jnp.float32)
        mean_square = jnp.mean(stream * stream, axis=-1, keepdims=True)
        normed_own = (stream * lax.rsqrt(mean_square + 1e-05) * norm_gain).astype(jnp.bfloat16)
        normed = lax.all_gather(normed_own, "exp", axis=0, tiled=True)

    with jax.named_scope("route"):
        chosen = expert_ids[0]
        share = CAP // exp_devices
        hits = (chosen[:, :, None] == jnp.arange(seq_devices, dtype=jnp.int32)).astype(jnp.float32)
        token_hits = jnp.sum(hits, axis=1)
        earlier = (
            jnp.arange(block_rows)[:, None] > jnp.arange(block_rows)[None, :]
        ).astype(jnp.float32)
        slots = jnp.dot(earlier, token_hits)
        named = token_hits[:, :, None] > 0
        wanted = (exp_rank * share + jnp.arange(share, dtype=jnp.int32)).astype(jnp.float32)
        picks = named & (slots[:, :, None] == wanted)
        selector = picks.astype(jnp.bfloat16).reshape(block_rows, seq_devices * share).T
        factor = jnp.einsum("tke,tk->te", hits, expert_gates[0].astype(jnp.float32))
        combiner = jnp.where(picks, factor[:, :, None], 0.0).astype(jnp.bfloat16)
        chunks = -(-width // CHUNK)
        combiner = combiner.reshape(block_rows, seq_devices * share)

    with jax.named_scope("dispatch"):
        outgoing = run_select(selector, normed).reshape(seq_devices, chunks * share, CHUNK)
        arrived = lax.all_to_all(outgoing, "seq", split_axis=0, concat_axis=0, tiled=True)

    with jax.named_scope("experts"):
        done = run_expert(arrived.reshape(seq_devices * chunks * share, CHUNK), weights)

    with jax.named_scope("combine"):
        returned = lax.all_to_all(
            done.reshape(seq_devices, chunks * share, CHUNK),
            "seq",
            split_axis=0,
            concat_axis=0,
            tiled=True,
        )
        term = run_combine(
            combiner, returned.reshape(seq_devices * chunks * share, CHUNK), width
        )
        terms = lax.all_to_all(
            term.reshape(exp_devices, own_rows, width),
            "exp",
            split_axis=0,
            concat_axis=0,
            tiled=True,
        )
        expert_sum = jnp.sum(terms.astype(jnp.float32), axis=0)
        layer_out = (residual.astype(jnp.float32) + expert_sum).astype(jnp.bfloat16)
    return layer_out[None]


def solution(mesh):
    placed = (
        P("batch", "seq", "exp"),
        P("batch", "seq", "exp"),
        P("exp"),
        P("exp", None),
        P("batch", ("seq", "exp"), None),
        P(),
        P("batch", "seq", None),
        P("batch", "seq", None),
        P("seq", None, "exp"),
        P("seq", None, "exp"),
        P("seq", "exp", None),
    )
    return jax.shard_map(
        on_device,
        mesh=mesh,
        in_specs=placed,
        out_specs=P("batch", ("seq", "exp"), None),
        check_vma=False,
    )
```

time: 252 us -> 243 us (0.964)
  local copies, waits for them, and re-layouts: 32 us -> 2.23 us
  waiting for transfers between devices: 60.1 us -> 81.4 us
  starting transfers between devices: 27.7 us -> 36.5 us
  blocking collectives: 86.7 us -> 79.8 us
  Pallas kernels: 15.3 us -> 20.8 us
  other arithmetic: 9.36 us -> 4.55 us
    all_to_all x1, waiting for transfers between devices: 6.03 us -> 35.1 us  [on_device(): lax.all_to_all(done.reshape(seq_devices, chunks * share, CHUNK), 'seq', s...]
    mul x1 -> x0, local copies, waits for them, and re-layouts: 22.1 us -> none  [on_device(): by_owner * same]
    all_to_all x1, waiting for transfers between devices: 21 us -> 12.4 us  [on_device(): lax.all_to_all(pair, 'exp', split_axis=0, concat_axis=0, tiled=True, axis...]
    all_to_all x1, blocking collectives: 55.9 us -> 48.2 us  [on_device(): lax.all_to_all(outgoing, 'seq', split_axis=0, concat_axis=0, tiled=True)]
    all_to_all x1, starting transfers between devices: 4.58 us -> 11.1 us  [on_device(): lax.all_to_all(done.reshape(seq_devices, chunks * share, CHUNK), 'seq', s...]
    unnamed x27 -> x17, local copies, waits for them, and re-layouts: 5.63 us -> 0.14 us
    mul x1 -> x0, other arithmetic: 5.43 us -> none  [on_device(): by_owner * same]
    pallas_call x1, Pallas kernels: 0.27 us -> 3.92 us  [pack_weights(): pl.pallas_call(pack_kernel, out_shape=jax.ShapeDtypeStruct((depth, width)...]
  transfers between devices with their start and end apart: 5 -> 6, of which waited for: 4 -> 5; matrix products, arithmetic and copies ran while one was open for 16% -> 4% of each run, Pallas kernels for 0% -> 0%
where the time goes in v3:
time: 243 us
  waiting for transfers between devices  81.4 us (33%)
  blocking collectives  79.8 us (33%)
  starting transfers between devices  36.5 us (15%)
  Pallas kernels  20.8 us (9%)
  between operations  13.7 us (6%)
  other arithmetic  4.55 us (2%)
  matrix products  3.79 us (2%)
    all_to_all x1, blocking collectives, on_device(): lax.all_to_all(outgoing, 'seq', split_axis=0, concat_axis=0, tiled=True)  48.2 us
    all_to_all x1, waiting for transfers between devices, on_device(): lax.all_to_all(done.reshape(seq_devices, chunks * share, CHUNK), 'seq', s...  35.1 us
    all_to_all x1, waiting for transfers between devices, on_device(): lax.all_to_all(copies, 'seq', split_axis=0, concat_axis=0, tiled=True, ax...  26.6 us
    all_to_all x1, blocking collectives, on_device(): lax.all_to_all(term.reshape(exp_devices, own_rows, width), 'exp', split_a...  16.7 us
    pallas_call x1, Pallas kernels, run_expert(): pl.pallas_call(expert_kernel, grid=(groups,), in_specs=[pl.BlockSpec((cou...  15.6 us
    all_to_all x1, starting transfers between devices, on_device(): lax.all_to_all(copies, 'seq', split_axis=0, concat_axis=0, tiled=True, ax...  15.2 us
    all_gather x1, blocking collectives, on_device(): normed = lax.all_gather(normed_own, 'exp', axis=0, tiled=True)  15 us
    all_to_all x1, waiting for transfers between devices, on_device(): lax.all_to_all(pair, 'exp', split_axis=0, concat_axis=0, tiled=True, axis...  12.4 us
  transfers between devices with their start and end apart: 6, of which 5 were waited for; matrix products, arithmetic and copies ran while one was open for 4% of the time, Pallas kernels for 0%

profile of v3, /device:TPU:32, one launch (start us, length us, event | category | flops | bytes accessed | tf_op | source)
XLA Modules:
  0.0 242.9 jit_solution(5988384783056664060)
XLA Ops:
  6.5 3.9 %gather_weights.1 = bf16[548,2880]{1,0:T(8,128)(2,1)} custom-call(bf16[180,2880]{1,0:T(8,128)(2,1)} %bitcast.145, bf16[180,2880]{1,0:T(8,128)(2,1)} %bitcast.146, bf16[180,2880]{1,0:T(8,128)(2,1)} %bitcast.147), custom_call_target="tpu_custom_call" | custom-call | bytes 6312960 | tf_op jit(solution)/shard_map/gather_weights/pallas_call | solution.py:26
  10.6 0.9 broadcast_in_dim.28
  11.5 15.2 %all-to-all-start = ((bf16[16,128,128]{1,2,0:T(8,128)(2,1)}), bf16[16,128,128]{1,2,0:T(8,128)(2,1)S(1)}, u32[]{:S(2)}, u32[]{:S(2)}) async-start(bf16[16,128,128]{1,2,0:T(8,128)(2,1)} %broadcast_in_dim.28), calls=%async_computation | async-start | bytes 1048576 | tf_op jit(solution)/shard_map/gather_keys/all_to_all | solution.py:222
  27.0 1.3 compare_and_fusion
  28.3 26.6 %all-to-all-done = bf16[16,128,128]{1,2,0:T(8,128)(2,1)S(1)} async-done(((bf16[16,128,128]{1,2,0:T(8,128)(2,1)}), bf16[16,128,128]{1,2,0:T(8,128)(2,1)S(1)}, u32[]{:S(2)}, u32[]{:S(2)}) %all-to-all-start) | async-done | bytes 524320 | tf_op jit(solution)/shard_map/gather_keys/all_to_all | solution.py:222
  55.1 3.4 %collective-permute-start = (bf16[2048,128]{0,1:T(8,128)(2,1)S(1)}, bf16[2048,128]{0,1:T(8,128)(2,1)S(1)}, u32[]{:S(2)}, u32[]{:S(2)}) collective-permute-start(bf16[2048,128]{0,1:T(8,128)(2,1)S(1)} %copy_bitcast_fusion), channel_id=1, source_target_pairs={{0,256},{16,272},{32,288},{48,304},{64,320},{80,336},{96,352},{112... | collective-permute-start | bytes 1572872 | tf_op jit(solution)/shard_map/gather_keys/ppermute | solution.py:226
  58.5 0.7 fusion.48
  59.3 0.6 fusion
  59.8 5.8 %collective-permute-done = bf16[2048,128]{0,1:T(8,128)(2,1)S(1)} collective-permute-done((bf16[2048,128]{0,1:T(8,128)(2,1)S(1)}, bf16[2048,128]{0,1:T(8,128)(2,1)S(1)}, u32[]{:S(2)}, u32[]{:S(2)}) %collective-permute-start) | collective-permute-done | bytes 524320 | tf_op jit(solution)/shard_map/gather_keys/ppermute | solution.py:226
  65.6 0.7 fusion.49
  66.4 0.6 fusion.2
  67.0 0.8 fusion.15
  67.8 0.8 fusion.30
  68.6 0.1 copy.47
  68.8 0.1 dot_general.33
  68.9 0.6 fusion.10
  69.6 1.9 collective-permute-start.1
  71.5 0.1 fusion.42
  71.7 1.5 collective-permute-done.1
  73.2 0.8 fusion.33
  74.0 4.8 %all-to-all-start.1 = ((bf16[4,16,2880]{2,1,0:T(8,128)(2,1)}), bf16[4,16,2880]{2,1,0:T(8,128)(2,1)S(1)}, u32[]{:S(2)}, u32[]{:S(2)}) async-start(bf16[4,16,2880]{2,1,0:T(8,128)(2,1)} %fusion.33), calls=%async_computation.1 | async-start | bytes 753664 | tf_op jit(solution)/shard_map/project/all_to_all | solution.py:274
  79.4 12.4 %all-to-all-done.1 = bf16[4,16,2880]{2,1,0:T(8,128)(2,1)S(1)} async-done(((bf16[4,16,2880]{2,1,0:T(8,128)(2,1)}), bf16[4,16,2880]{2,1,0:T(8,128)(2,1)S(1)}, u32[]{:S(2)}, u32[]{:S(2)}) %all-to-all-start.1) | async-done | bytes 368672 | tf_op jit(solution)/shard_map/project/all_to_all | solution.py:274
  91.8 0.2 fusion.38
  92.1 15.0 %all_gather.9.normed_ref = bf16[128,2880]{1,0:T(8,128)(2,1)S(1)} all-gather(bf16[16,2880]{1,0:T(8,128)(2,1)S(1)} %fusion.40), channel_id=1, replica_groups=mesh['seq'=32,'exp'=8,'batch'=2] {'exp'}, dimensions={0}, use_global_device_ids=true | all-gather | bytes 829440 | tf_op jit(solution)/shard_map/norm/all_gather | solution.py:284
  107.1 0.7 dispatch.1
  107.7 48.2 %all_to_all.25 = bf16[32,24,384]{2,1,0:T(8,128)(2,1)S(1)} all-to-all(bf16[32,24,384]{2,1,0:T(8,128)(2,1)S(1)} %bitcast.143), channel_id=1, replica_groups=mesh['seq'=32,'exp'=8,'batch'=2] {'seq'}, dimensions={0} | all-to-all | bytes 1179648 | tf_op jit(solution)/shard_map/dispatch/all_to_all | solution.py:306
  155.9 15.6 %experts.1 = bf16[768,384]{1,0:T(8,128)(2,1)} custom-call(bf16[768,384]{1,0:T(8,128)(2,1)S(1)} %bitcast.141, bf16[8,548,2880]{2,1,0:T(8,128)(2,1)} %all-gather.4.cloned.1.call-done.weight_ref), custom_call_target="tpu_custom_call" | custom-call | flops 2424176640 | bytes 25251840 | tf_op jit(solution)/shard_map/experts/pallas_call | solution.py:164
  171.5 11.1 %all-to-all-start.3 = ((bf16[32,24,384]{2,1,0:T(8,128)(2,1)}), bf16[32,24,384]{2,1,0:T(8,128)(2,1)S(1)}, u32[]{:S(2)}, u32[]{:S(2)}) async-start(bf16[32,24,384]{2,1,0:T(8,128)(2,1)} %bitcast.31), calls=%async_computation.3 | async-start | bytes 1179648 | tf_op jit(solution)/shard_map/combine/all_to_all | solution.py:312
  182.8 35.1 %all-to-all-done.3 = bf16[32,24,384]{2,1,0:T(8,128)(2,1)S(1)} async-done(((bf16[32,24,384]{2,1,0:T(8,128)(2,1)}), bf16[32,24,384]{2,1,0:T(8,128)(2,1)S(1)}, u32[]{:S(2)}, u32[]{:S(2)}) %all-to-all-start.3) | async-done | bytes 589856 | tf_op jit(solution)/shard_map/combine/all_to_all | solution.py:312
  217.9 0.7 combine.1
  218.5 16.7 %all_to_all.26 = bf16[8,16,2880]{2,1,0:T(8,128)(2,1)S(1)} all-to-all(bf16[8,16,2880]{2,1,0:T(8,128)(2,1)S(1)} %bitcast.140), channel_id=1, replica_groups=mesh['seq'=32,'exp'=8,'batch'=2] {'exp'}, dimensions={0} | all-to-all | bytes 1474560 | tf_op jit(solution)/shard_map/combine/all_to_all | solution.py:322
  235.3 0.7 fusion.41
  (48 shorter events, 1.5 us)
Async XLA Ops:
  6.5 62.4 %copy-start = (bf16[256,2880]{0,1:T(8,128)(2,1)S(1)}, bf16[256,2880]{0,1:T(8,128)(2,1)}, u32[]{:S(2)}) copy-start(bf16[256,2880]{0,1:T(8,128)(2,1)} %param.14) | copy-start | bytes 4423684
  6.5 149.4 %all-gather.4.cloned.1.call-start = ((), (), s32[]{:S(2)}) async-start(), calls=%async_computation.5 | async-start | bytes 29251584 | tf_op jit(solution)/shard_map/gather_weights/all_gather | solution.py:212
  6.5 4.0 %copy-start.3 = (bf16[1,128,128]{2,1,0:T(8,128)(2,1)S(1)}, bf16[1,128,128]{2,1,0:T(8,128)(2,1)}, u32[]{:S(2)}) copy-start(bf16[1,128,128]{2,1,0:T(8,128)(2,1)} %param.12) | copy-start | bytes 98308
  6.5 20.2 %copy-start.2 = (bf16[1,128,256]{2,1,0:T(8,128)(2,1)S(1)}, bf16[1,128,256]{2,1,0:T(8,128)(2,1)}, u32[]{:S(2)}) copy-start(bf16[1,128,256]{2,1,0:T(8,128)(2,1)} %param.11) | copy-start | bytes 196612
  10.5 16.5 %copy-start.6 = (bf16[1,128,4]{1,2,0:T(4,128)(2,1)S(1)}, bf16[1,128,4]{1,2,0:T(4,128)(2,1)}, u32[]{:S(2)}) copy-start(bf16[1,128,4]{1,2,0:T(4,128)(2,1)} %param.18) | copy-start | bytes 3076
  10.5 16.5 %copy-start.5 = (s32[1,128,4]{1,2,0:T(4,128)S(1)}, s32[1,128,4]{1,2,0:T(4,128)}, u32[]{:S(2)}) copy-start(s32[1,128,4]{1,2,0:T(4,128)} %param.17) | copy-start | bytes 6148
  11.5 43.4 %all-to-all-start = ((bf16[16,128,128]{1,2,0:T(8,128)(2,1)}), bf16[16,128,128]{1,2,0:T(8,128)(2,1)S(1)}, u32[]{:S(2)}, u32[]{:S(2)}) async-start(bf16[16,128,128]{1,2,0:T(8,128)(2,1)} %broadcast_in_dim.28), calls=%async_computation | async-start | bytes 1048576 | tf_op jit(solution)/shard_map/gather_keys/all_to_all | solution.py:222
  55.1 10.6 %collective-permute-start = (bf16[2048,128]{0,1:T(8,128)(2,1)S(1)}, bf16[2048,128]{0,1:T(8,128)(2,1)S(1)}, u32[]{:S(2)}, u32[]{:S(2)}) collective-permute-start(bf16[2048,128]{0,1:T(8,128)(2,1)S(1)} %copy_bitcast_fusion), channel_id=1, source_target_pairs={{0,256},{16,272},{32,288},{48,304},{64,320},{80,336},{96,352},{112... | collective-permute-start | bytes 1572872 | tf_op jit(solution)/shard_map/gather_keys/ppermute | solution.py:226
  65.6 1.3 copy-start.7
  68.6 23.2 %copy-start.1 = (bf16[1,16,2880]{2,1,0:T(8,128)(2,1)S(1)}, bf16[1,16,2880]{2,1,0:T(8,128)(2,1)}, u32[]{:S(2)}) copy-start(bf16[1,16,2880]{2,1,0:T(8,128)(2,1)} %param.15) | copy-start | bytes 276484
  68.6 23.4 %copy-start.4 = (f32[2880]{0:T(1024)S(1)}, f32[2880]{0:T(1024)}, u32[]{:S(2)}) copy-start(f32[2880]{0:T(1024)} %param.16) | copy-start | bytes 34564
  69.6 3.6 %collective-permute-start.1 = (bf16[4,16,2880]{2,1,0:T(8,128)(2,1)S(1)}, bf16[4,16,2880]{2,1,0:T(8,128)(2,1)S(1)}, u32[]{:S(2)}, u32[]{:S(2)}) collective-permute-start(bf16[4,16,2880]{2,1,0:T(8,128)(2,1)S(1)} %fusion.34), channel_id=1, source_target_pairs={{0,2},{2,0},{4,6},{6,4},{8,10},{10,8},{12,14},{14,12},{1,3},{3,1},... | collective-permute-start | bytes 1105928 | tf_op jit(solution)/shard_map/project/ppermute | solution.py:269
  74.0 17.8 %all-to-all-start.1 = ((bf16[4,16,2880]{2,1,0:T(8,128)(2,1)}), bf16[4,16,2880]{2,1,0:T(8,128)(2,1)S(1)}, u32[]{:S(2)}, u32[]{:S(2)}) async-start(bf16[4,16,2880]{2,1,0:T(8,128)(2,1)} %fusion.33), calls=%async_computation.1 | async-start | bytes 753664 | tf_op jit(solution)/shard_map/project/all_to_all | solution.py:274
  171.5 46.4 %all-to-all-start.3 = ((bf16[32,24,384]{2,1,0:T(8,128)(2,1)}), bf16[32,24,384]{2,1,0:T(8,128)(2,1)S(1)}, u32[]{:S(2)}, u32[]{:S(2)}) async-start(bf16[32,24,384]{2,1,0:T(8,128)(2,1)} %bitcast.31), calls=%async_computation.3 | async-start | bytes 1179648 | tf_op jit(solution)/shard_map/combine/all_to_all | solution.py:312
Sparse Core Ops, SparseCore 0:
  10.6 142.6 all-gather.3

commit v4 on v3

v4 whole, which is shorter than its diff:
```python
import jax
import jax.numpy as jnp
from jax import lax
from jax.experimental import pallas as pl
from jax.experimental.pallas import tpu as pltpu
from jax.sharding import PartitionSpec as P

HEAD = 64
TILE = 16
CHUNK = 384
CAP = 24
GROUP = 24
CORES = 2
RUN = 16


def pack_kernel(gate_ref, up_ref, down_ref, out_ref):
    out_ref[...] = jnp.concatenate([gate_ref[...], up_ref[...], down_ref[...]], axis=0)


def pack_weights(gate_across, up_across, down):
    units, width = down.shape
    depth = 3 * units
    return pl.pallas_call(
        pack_kernel,
        out_shape=jax.ShapeDtypeStruct((depth, width), down.dtype),
        compiler_params=pltpu.CompilerParams(vmem_limit_bytes=56 * 1024 * 1024),
        cost_estimate=pl.CostEstimate(
            flops=0, bytes_accessed=4 * depth * width, transcendentals=0
        ),
    )(gate_across, up_across, down)


def chunk_turn(chunks, back):
    side = GROUP * chunks
    share = CAP // chunks
    row = lax.broadcasted_iota(jnp.int32, (side, side), 1 if back else 0)
    col = lax.broadcasted_iota(jnp.int32, (side, side), 0 if back else 1)
    block, rest = row // (chunks * share), row % (chunks * share)
    source = (rest // share) * GROUP + block * share + rest % share
    return (source == col).astype(jnp.bfloat16)


def store_chunks(rows_ref, out_ref):
    count, width = rows_ref.shape
    chunks = out_ref.shape[0] // count
    turn = chunk_turn(chunks, False)
    for first in range(0, count, GROUP):
        pieces = []
        for chunk in range(chunks):
            low, high = chunk * CHUNK, min((chunk + 1) * CHUNK, width)
            piece = rows_ref[first : first + GROUP, low:high]
            if high - low < CHUNK:
                fill = jnp.zeros((GROUP, CHUNK - (high - low)), piece.dtype)
                piece = jnp.concatenate([piece, fill], axis=1)
            pieces.append(piece)
        stacked = jnp.concatenate(pieces, axis=0).astype(jnp.bfloat16)
        out_ref[first * chunks : (first + GROUP) * chunks, :] = jnp.dot(
            turn, stacked, preferred_element_type=jnp.float32
        ).astype(out_ref.dtype)


def load_chunks(chunks_ref, count):
    chunks = chunks_ref.shape[0] // count
    turn = chunk_turn(chunks, True)
    rows = []
    for first in range(0, count, GROUP):
        stacked = jnp.dot(
            turn,
            chunks_ref[first * chunks : (first + GROUP) * chunks, :],
            preferred_element_type=jnp.float32,
        )
        rows.append(
            jnp.concatenate([stacked[i * GROUP : (i + 1) * GROUP] for i in range(chunks)], axis=1)
        )
    return jnp.concatenate(rows, axis=0)


def combine_kernel(combiner_ref, chunks_ref, out_ref):
    width = out_ref.shape[1]
    rows = load_chunks(chunks_ref, combiner_ref.shape[1])[:, :width].astype(jnp.bfloat16)
    out_ref[...] = jnp.dot(
        combiner_ref[...], rows, preferred_element_type=jnp.float32
    ).astype(out_ref.dtype)


def run_combine(combiner, chunk_rows, width):
    tokens, count = combiner.shape
    return pl.pallas_call(
        combine_kernel,
        out_shape=jax.ShapeDtypeStruct((tokens, width), jnp.bfloat16),
        compiler_params=pltpu.CompilerParams(vmem_limit_bytes=24 * 1024 * 1024),
        cost_estimate=pl.CostEstimate(
            flops=2 * tokens * count * width, bytes_accessed=4 * tokens * width, transcendentals=0
        ),
    )(combiner, chunk_rows)


def select_kernel(selector_ref, normed_ref, out_ref, rows_ref):
    rows_ref[...] = jnp.dot(
        selector_ref[...], normed_ref[...], preferred_element_type=jnp.float32
    )
    store_chunks(rows_ref, out_ref)


def run_select(selector, normed):
    count, depth = selector.shape
    width = normed.shape[1]
    chunks = -(-width // CHUNK)
    return pl.pallas_call(
        select_kernel,
        out_shape=jax.ShapeDtypeStruct((count * chunks, CHUNK), jnp.bfloat16),
        scratch_shapes=[pltpu.VMEM((count, width), jnp.float32)],
        compiler_params=pltpu.CompilerParams(vmem_limit_bytes=24 * 1024 * 1024),
        cost_estimate=pl.CostEstimate(
            flops=4 * count * depth * width, bytes_accessed=4 * count * width, transcendentals=0
        ),
    )(selector, normed)


def group_term(weight_ref, rows_across):
    units = weight_ref.shape[0] // 3
    count = rows_across.shape[1]
    lift_rows = -(-2 * units // TILE) * TILE
    down_from = 2 * units // TILE * TILE
    cut = lift_rows // (2 * TILE) * TILE
    both = jnp.concatenate(
        [
            jnp.dot(weight_ref[:cut, :], rows_across, preferred_element_type=jnp.float32),
            jnp.dot(
                weight_ref[cut:lift_rows, :], rows_across, preferred_element_type=jnp.float32
            ),
        ],
        axis=0,
    )
    gate = both[:units]
    lifted = both[units : 2 * units]
    hidden = gate * jax.nn.sigmoid(1.702 * gate) * (lifted + 1.0)
    lead = jnp.zeros((2 * units - down_from, count), jnp.float32)
    hidden = jnp.concatenate([lead, hidden], axis=0)
    return jnp.dot(
        hidden.T.astype(jnp.bfloat16),
        weight_ref[down_from:, :],
        preferred_element_type=jnp.float32,
    )


def peer_kernel(chunks_ref, peer_ref, total_ref, held_ref, sem):
    count, width = total_ref.shape
    copy = pltpu.make_async_copy(peer_ref, held_ref, sem)
    copy.start()
    rows_across = load_chunks(chunks_ref, count).T[:width].astype(jnp.bfloat16)
    copy.wait()
    total_ref[...] = group_term(held_ref, rows_across)


def run_peer(chunk_rows, peer):
    depth, width = peer.shape
    count = chunk_rows.shape[0] // -(-width // CHUNK)
    return pl.pallas_call(
        peer_kernel,
        in_specs=[
            pl.BlockSpec(memory_space=pltpu.VMEM),
            pl.BlockSpec(memory_space=pl.ANY),
        ],
        out_specs=pl.BlockSpec(memory_space=pltpu.VMEM),
        out_shape=jax.ShapeDtypeStruct((count, width), jnp.float32),
        scratch_shapes=[
            pltpu.VMEM((depth, width), jnp.bfloat16),
            pltpu.SemaphoreType.DMA,
        ],
        compiler_params=pltpu.CompilerParams(vmem_limit_bytes=24 * 1024 * 1024),
        cost_estimate=pl.CostEstimate(
            flops=2 * count * width * depth,
            bytes_accessed=2 * depth * width,
            transcendentals=count * depth // 3,
        ),
    )(chunk_rows, peer)


def expert_kernel(
    chunks_ref, start_ref, weight_ref, out_ref, held_ref, total_ref, ready_ref, sems, out_sems
):
    groups = weight_ref.shape[0]
    others = held_ref.shape[0]
    count, width = total_ref.shape
    rank = lax.axis_index("exp")
    first = rank // CORES * CORES + CORES

    def fetch(i):
        group = lax.rem(first + i, groups) if i < groups - CORES else rank
        return pltpu.make_async_copy(weight_ref.at[group], held_ref.at[i], sems.at[i])

    for i in range(others):
        fetch(i).start()
    total_ref[...] = start_ref[...]
    rows_across = load_chunks(chunks_ref, count).T[:width].astype(jnp.bfloat16)
    for i in range(others):
        fetch(i).wait()
        total_ref[...] += group_term(held_ref.at[i], rows_across)
    store_chunks(total_ref, ready_ref)
    copy = pltpu.make_async_copy(ready_ref, out_ref, out_sems)
    copy.start()
    copy.wait()


def run_expert(chunk_rows, start, weights):
    groups, depth, width = weights.shape
    count = start.shape[0]
    others = groups - 1
    return pl.pallas_call(
        expert_kernel,
        in_specs=[
            pl.BlockSpec(memory_space=pltpu.VMEM),
            pl.BlockSpec(memory_space=pltpu.VMEM),
            pl.BlockSpec(memory_space=pl.ANY),
        ],
        out_specs=pl.BlockSpec(memory_space=pltpu.HBM),
        out_shape=jax.ShapeDtypeStruct(chunk_rows.shape, jnp.bfloat16),
        scratch_shapes=[
            pltpu.VMEM((others, depth, width), jnp.bfloat16),
            pltpu.VMEM((count, width), jnp.float32),
            pltpu.VMEM(chunk_rows.shape, jnp.bfloat16),
            pltpu.SemaphoreType.DMA((others,)),
            pltpu.SemaphoreType.DMA,
        ],
        compiler_params=pltpu.CompilerParams(vmem_limit_bytes=44 * 1024 * 1024),
        cost_estimate=pl.CostEstimate(
            flops=2 * count * width * depth * others,
            bytes_accessed=others * depth * width * 2,
            transcendentals=count * depth * others // 3,
        ),
    )(chunk_rows, start, weights)


def on_device(
    queries,
    keys_values,
    sinks,
    out_weight,
    hidden_in,
    norm_gain,
    expert_ids,
    expert_gates,
    gate_weight,
    up_weight,
    down_weight,
):
    seq_devices = lax.axis_size("seq")
    exp_devices = lax.axis_size("exp")
    block_rows = queries.shape[1]
    heads = sinks.shape[0]
    width = out_weight.shape[1]
    own_rows = hidden_in.shape[1]
    units = gate_weight.shape[2]
    seq_rank = lax.axis_index("seq")
    exp_rank = lax.axis_index("exp")
    run_rows = RUN * block_rows
    runs = seq_devices // RUN

    with jax.named_scope("gather_weights"):
        weights_own = pack_weights(gate_weight[0].T, up_weight[0].T, down_weight[0])
        weights = lax.all_gather(weights_own, "exp", axis=0, tiled=False)
        swap = [(i, i ^ 1) for i in range(exp_devices)]
        weights_peer = lax.ppermute(weights_own, "exp", swap)

    with jax.named_scope("gather_keys"):
        run_groups = [[r * RUN + i for i in range(RUN)] for r in range(runs)]
        copies = jnp.broadcast_to(keys_values, (RUN,) + keys_values.shape[1:])
        near = lax.all_to_all(
            copies, "seq", split_axis=0, concat_axis=0, tiled=True, axis_index_groups=run_groups
        )
        near = near.reshape(run_rows, 2 * HEAD)
        to_far = [(i, i + RUN) for i in range(seq_devices - RUN)]
        to_near = [(i + RUN, i) for i in range(seq_devices - RUN)]
        guests = lax.ppermute(queries[0], "seq", to_near)

    with jax.named_scope("route"):
        chips = exp_devices // CORES
        core = exp_rank % CORES
        chosen = expert_ids[0]
        share = CAP // exp_devices
        hits = (chosen[:, :, None] == jnp.arange(seq_devices, dtype=jnp.int32)).astype(jnp.float32)
        token_hits = jnp.sum(hits, axis=1)
        earlier = (
            jnp.arange(block_rows)[:, None] > jnp.arange(block_rows)[None, :]
        ).astype(jnp.float32)
        slots = jnp.dot(earlier, token_hits)
        named = token_hits[:, :, None] > 0
        wanted = (exp_rank * share + jnp.arange(share, dtype=jnp.int32)).astype(jnp.float32)
        picks = named & (slots[:, :, None] == wanted)
        selector = picks.astype(jnp.bfloat16).reshape(
            chips, CORES, own_rows, seq_devices * share
        )
        selector = selector.transpose(3, 1, 0, 2).reshape(seq_devices * share, block_rows)
        factor = jnp.einsum("tke,tk->te", hits, expert_gates[0].astype(jnp.float32))
        combiner = jnp.where(picks, factor[:, :, None], 0.0).astype(jnp.bfloat16)
        chunks = -(-width // CHUNK)
        combiner = combiner.reshape(block_rows, seq_devices * share)
        selector, combiner, near = lax.optimization_barrier((selector, combiner, near))

    with jax.named_scope("attend"):
        grid = jnp.concatenate([queries[0], guests], axis=0)
        grid = grid.reshape(2 * block_rows, heads, HEAD)
        own_pos = (seq_rank % RUN) * block_rows + jnp.arange(block_rows, dtype=jnp.int32)
        query_pos = jnp.concatenate([own_pos, jnp.full((block_rows,), run_rows, jnp.int32)])
        key_pos = jnp.arange(run_rows, dtype=jnp.int32)
        scores = (
            jnp.einsum("igd,jd->gij", grid, near[:, :HEAD], preferred_element_type=jnp.float32)
            * 0.125
        )
        scores = jnp.where(key_pos[None, :] <= query_pos[:, None], scores, -1e30)
        top = jnp.max(scores, axis=-1)
        numerators = jnp.exp(scores - top[..., None])
        sums = jnp.sum(numerators, axis=-1)
        weighted = jnp.einsum(
            "gij,jd->gid",
            numerators.astype(jnp.bfloat16),
            near[:, HEAD:],
            preferred_element_type=jnp.float32,
        )
        guest_stats = jnp.stack([top[:, block_rows:], sums[:, block_rows:]])
        guest_mix = weighted[:, block_rows:].astype(jnp.bfloat16)
        far_stats = lax.ppermute(guest_stats, "seq", to_far)
        far_mix = lax.ppermute(guest_mix, "seq", to_far)
        top, sums, weighted = top[:, :block_rows], sums[:, :block_rows], weighted[:, :block_rows]
        far_top = jnp.where(seq_rank >= RUN, far_stats[0], -1e30)
        largest = jnp.maximum(jnp.maximum(top, far_top), sinks[:, None])
        near_scale = jnp.exp(top - largest)
        far_scale = jnp.exp(far_top - largest)
        totals = (
            sums * near_scale + far_stats[1] * far_scale + jnp.exp(sinks[:, None] - largest)
        )
        weighted = (
            weighted * near_scale[..., None]
            + far_mix.astype(jnp.float32) * far_scale[..., None]
        )
        mixed = (weighted / totals[..., None]).astype(jnp.bfloat16)
        heads_out = mixed.transpose(1, 0, 2).reshape(block_rows, heads * HEAD)

    with jax.named_scope("project"):
        head_term = jnp.dot(heads_out, out_weight, preferred_element_type=jnp.float32)
        head_parts = head_term.reshape(chips, CORES, own_rows, width)
        given = lax.dynamic_index_in_dim(head_parts, 1 - core, 1, keepdims=False)
        kept = lax.dynamic_index_in_dim(head_parts, core, 1, keepdims=False)
        taken = lax.ppermute(given.astype(jnp.bfloat16), "exp", swap)
        pair = (kept + taken.astype(jnp.float32)).astype(jnp.bfloat16)
        columns = [[CORES * i + c for i in range(chips)] for c in range(CORES)]
        own_parts = lax.all_to_all(
            pair, "exp", split_axis=0, concat_axis=0, tiled=True, axis_index_groups=columns
        )
        attention = jnp.sum(own_parts.astype(jnp.float32), axis=0)
        residual = (hidden_in[0].astype(jnp.float32) + attention).astype(jnp.bfloat16)

    with jax.named_scope("norm"):
        stream = residual.astype(jnp.float32)
        mean_square = jnp.mean(stream * stream, axis=-1, keepdims=True)
        normed_own = (stream * lax.rsqrt(mean_square + 1e-05) * norm_gain).astype(jnp.bfloat16)
        normed_own, weights_peer = lax.optimization_barrier((normed_own, weights_peer))
        normed = lax.all_gather(
            normed_own, "exp", axis=0, tiled=True, axis_index_groups=columns
        )
        cores = [[CORES * i + c for c in range(CORES)] for i in range(chips)]
        normed = lax.all_gather(normed, "exp", axis=0, tiled=True, axis_index_groups=cores)

    with jax.named_scope("dispatch"):
        outgoing = run_select(selector, normed).reshape(seq_devices, chunks * share, CHUNK)
        arrived = lax.all_to_all(outgoing, "seq", split_axis=0, concat_axis=0, tiled=True)

    with jax.named_scope("experts"):
        chunk_rows = arrived.reshape(seq_devices * chunks * share, CHUNK)
        start = run_peer(chunk_rows, weights_peer)
        done = run_expert(chunk_rows, start, weights)

    with jax.named_scope("combine"):
        returned = lax.all_to_all(
            done.reshape(seq_devices, chunks * share, CHUNK),
            "seq",
            split_axis=0,
            concat_axis=0,
            tiled=True,
        )
        term = run_combine(
            combiner, returned.reshape(seq_devices * chunks * share, CHUNK), width
        )
        terms = lax.all_to_all(
            term.reshape(exp_devices, own_rows, width),
            "exp",
            split_axis=0,
            concat_axis=0,
            tiled=True,
        )
        expert_sum = jnp.sum(terms.astype(jnp.float32), axis=0)
        layer_out = (residual.astype(jnp.float32) + expert_sum).astype(jnp.bfloat16)
    return layer_out[None]


def solution(mesh):
    placed = (
        P("batch", "seq", "exp"),
        P("batch", "seq", "exp"),
        P("exp"),
        P("exp", None),
        P("batch", ("seq", "exp"), None),
        P(),
        P("batch", "seq", None),
        P("batch", "seq", None),
        P("seq", None, "exp"),
        P("seq", None, "exp"),
        P("seq", "exp", None),
    )
    return jax.shard_map(
        on_device,
        mesh=mesh,
        in_specs=placed,
        out_specs=P("batch", ("seq", "exp"), None),
        check_vma=False,
    )
```

time: 243 us -> 236 us (0.971)
  waiting for transfers between devices: 81.4 us -> 38.6 us
  blocking collectives: 79.8 us -> 122 us
  starting transfers between devices: 36.5 us -> 30.1 us
    all_to_all x0 -> x1, blocking collectives: none -> 44.3 us  [on_device(): lax.all_to_all(done.reshape(seq_devices, chunks * share, CHUNK), 'seq', s...]
    all_to_all x1 -> x0, waiting for transfers between devices: 35.1 us -> none  [on_device(): lax.all_to_all(done.reshape(seq_devices, chunks * share, CHUNK), 'seq', s...]
    all_to_all x1 -> x0, starting transfers between devices: 11.1 us -> none  [on_device(): lax.all_to_all(done.reshape(seq_devices, chunks * share, CHUNK), 'seq', s...]
    all_to_all x1, waiting for transfers between devices: 26.6 us -> 19.8 us  [on_device(): lax.all_to_all(copies, 'seq', split_axis=0, concat_axis=0, tiled=True, ax...]
    all_to_all x1, blocking collectives: 48.2 us -> 43.5 us  [on_device(): lax.all_to_all(outgoing, 'seq', split_axis=0, concat_axis=0, tiled=True)]
    ppermute x2 -> x5, starting transfers between devices: 5.35 us -> 9.92 us  [the longest x1 3.52 us: on_device(): far_stats = lax.ppermute(guest_stats, 'seq', to_far)]
    pallas_call x1 -> x2, Pallas kernels: 15.6 us -> 13.4 us  [the longest x1 10.3 us: run_expert(): pl.pallas_call(expert_kernel, in_specs=[pl.BlockSpec(memory_space=pltpu.V...]
    all_gather x1 -> x2, blocking collectives: 15 us -> 17.1 us  [the longest x1 14.3 us: on_device(): lax.all_gather(normed_own, 'exp', axis=0, tiled=True, axis_index_groups=c...]
  transfers between devices with their start and end apart: 6 -> 8, of which waited for: 5 -> 5; matrix products, arithmetic and copies ran while one was open for 4% -> 5% of each run, Pallas kernels for 0% -> 2%
where the time goes in v4:
time: 236 us
  blocking collectives  122 us (52%)
  waiting for transfers between devices  38.6 us (16%)
  starting transfers between devices  30.1 us (13%)
  Pallas kernels  18.7 us (8%)
  between operations  13.9 us (6%)
  other arithmetic  4.67 us (2%)
  matrix products  4.3 us (2%)
  local copies, waits for them, and re-layouts  4.11 us (2%)
    all_to_all x1, blocking collectives, on_device(): lax.all_to_all(done.reshape(seq_devices, chunks * share, CHUNK), 'seq', s...  44.3 us
    all_to_all x1, blocking collectives, on_device(): lax.all_to_all(outgoing, 'seq', split_axis=0, concat_axis=0, tiled=True)  43.5 us
    all_to_all x1, waiting for transfers between devices, on_device(): lax.all_to_all(copies, 'seq', split_axis=0, concat_axis=0, tiled=True, ax...  19.8 us
    all_to_all x1, blocking collectives, on_device(): lax.all_to_all(term.reshape(exp_devices, own_rows, width), 'exp', split_a...  16.7 us
    all_to_all x1, starting transfers between devices, on_device(): lax.all_to_all(copies, 'seq', split_axis=0, concat_axis=0, tiled=True, ax...  15.2 us
    all_gather x1, blocking collectives, on_device(): lax.all_gather(normed_own, 'exp', axis=0, tiled=True, axis_index_groups=c...  14.3 us
    all_to_all x1, waiting for transfers between devices, on_device(): lax.all_to_all(pair, 'exp', split_axis=0, concat_axis=0, tiled=True, axis...  12.8 us
    pallas_call x1, Pallas kernels, run_expert(): pl.pallas_call(expert_kernel, in_specs=[pl.BlockSpec(memory_space=pltpu.V...  10.3 us
  transfers between devices with their start and end apart: 8, of which 5 were waited for; matrix products, arithmetic and copies ran while one was open for 5% of the time, Pallas kernels for 2%

profile of v4, /device:TPU:32, one launch (start us, length us, event | category | flops | bytes accessed | tf_op | source)
XLA Modules:
  0.0 235.8 jit_solution(9150732253675165910)
XLA Ops:
  6.6 3.9 %gather_weights.1 = bf16[540,2880]{1,0:T(8,128)(2,1)} custom-call(bf16[180,2880]{1,0:T(8,128)(2,1)} %bitcast.115, bf16[180,2880]{1,0:T(8,128)(2,1)} %bitcast.116, bf16[180,2880]{1,0:T(8,128)(2,1)} %bitcast.117), custom_call_target="tpu_custom_call" | custom-call | bytes 6220800 | tf_op jit(solution)/shard_map/gather_weights/pallas_call | solution.py:24
  10.7 0.9 broadcast_in_dim.35
  11.6 15.2 %all-to-all-start = ((bf16[16,128,128]{1,2,0:T(8,128)(2,1)}), bf16[16,128,128]{1,2,0:T(8,128)(2,1)S(1)}, u32[]{:S(2)}, u32[]{:S(2)}) async-start(bf16[16,128,128]{1,2,0:T(8,128)(2,1)} %broadcast_in_dim.35), calls=%async_computation | async-start | bytes 1048576 | tf_op jit(solution)/shard_map/gather_keys/all_to_all | solution.py:270
  26.8 1.9 collective-permute-start.4
  28.7 1.3 collective-permute-start
  30.6 0.5 eq.50
  31.8 0.4 fusion.15
  32.8 2.3 collective-permute-done
  35.2 19.8 %all-to-all-done = bf16[16,128,128]{1,2,0:T(8,128)(2,1)S(1)} async-done(((bf16[16,128,128]{1,2,0:T(8,128)(2,1)}), bf16[16,128,128]{1,2,0:T(8,128)(2,1)S(1)}, u32[]{:S(2)}, u32[]{:S(2)}) %all-to-all-start) | async-done | bytes 524320 | tf_op jit(solution)/shard_map/gather_keys/all_to_all | solution.py:270
  55.1 1.5 fusion.2
  56.6 1.8 fusion
  58.5 3.5 %collective-permute-start.1 = (f32[2,4,128]{2,1,0:T(4,128)S(1)}, f32[2,4,128]{2,1,0:T(4,128)S(1)}, u32[]{:S(2)}, u32[]{:S(2)}) collective-permute-start(f32[2,4,128]{2,1,0:T(4,128)S(1)} %pad_maximum_fusion), channel_id=1, source_target_pairs={{0,256},{16,272},{32,288},{48,304},{64,320},{80,336},{96,352},{112... | collective-permute-start | bytes 12296 | tf_op jit(solution)/shard_map/attend/ppermute | solution.py:324
  62.0 2.1 fusion.3
  64.1 1.3 collective-permute-start.2
  65.6 1.7 collective-permute-done.2
  67.6 0.6 fusion.6
  68.2 0.8 fusion.9
  69.0 1.9 collective-permute-start.3
  71.0 1.9 collective-permute-done.3
  72.8 0.8 fusion.8
  73.6 4.9 %all-to-all-start.1 = ((bf16[4,16,2880]{2,1,0:T(8,128)(2,1)}), bf16[4,16,2880]{2,1,0:T(8,128)(2,1)S(1)}, u32[]{:S(2)}, u32[]{:S(2)}) async-start(bf16[4,16,2880]{2,1,0:T(8,128)(2,1)} %fusion.8), calls=%async_computation.1 | async-start | bytes 753664 | tf_op jit(solution)/shard_map/project/all_to_all | solution.py:349
  78.6 12.8 %all-to-all-done.1 = bf16[4,16,2880]{2,1,0:T(8,128)(2,1)S(1)} async-done(((bf16[4,16,2880]{2,1,0:T(8,128)(2,1)}), bf16[4,16,2880]{2,1,0:T(8,128)(2,1)S(1)}, u32[]{:S(2)}, u32[]{:S(2)}) %all-to-all-start.1) | async-done | bytes 368672 | tf_op jit(solution)/shard_map/project/all_to_all | solution.py:349
  91.8 14.3 %all_gather.12 = bf16[64,2880]{1,0:T(8,128)(2,1)S(1)} all-gather(bf16[16,2880]{1,0:T(8,128)(2,1)S(1)} %fusion.21), channel_id=1, replica_groups={{0,4,8,12},{2,6,10,14},{1,5,9,13},{3,7,11,15},{16,20,24,28},{18,22,26,3..., dimensions={0}, use_global_device_ids=true | all-gather | bytes 460800 | tf_op jit(solution)/shard_map/norm/all_gather | solution.py:360
  106.1 2.7 %all_gather.13.normed_ref = bf16[128,2880]{1,0:T(8,128)(2,1)S(1)} all-gather(bf16[64,2880]{1,0:T(8,128)(2,1)S(1)} %all_gather.12), channel_id=1, replica_groups={{0,2},{4,6},{8,10},{12,14},{1,3},{5,7},{9,11},{13,15},{16,18},{20,22},{..., dimensions={0}, use_global_device_ids=true | all-gather | bytes 1105920 | tf_op jit(solution)/shard_map/norm/all_gather | solution.py:364
  108.9 0.7 dispatch.1
  109.6 43.5 %all_to_all.25 = bf16[32,24,384]{2,1,0:T(8,128)(2,1)S(1)} all-to-all(bf16[32,24,384]{2,1,0:T(8,128)(2,1)S(1)} %bitcast.112), channel_id=1, replica_groups=mesh['seq'=32,'exp'=8,'batch'=2] {'seq'}, dimensions={0} | all-to-all | bytes 1179648 | tf_op jit(solution)/shard_map/dispatch/all_to_all | solution.py:368
  153.1 3.2 %experts.2.start_ref = f32[96,2880]{1,0:T(8,128)S(1)} custom-call(bf16[768,384]{1,0:T(8,128)(2,1)S(1)} %bitcast.108, bf16[540,2880]{1,0:T(8,128)(2,1)} %collective-permute-done.4.peer_ref), custom_call_target="tpu_custom_call" | custom-call | flops 298598400 | bytes 3110400 | tf_op jit(solution)/shard_map/experts/pallas_call | solution.py:160
  156.3 10.3 %experts.3 = bf16[768,384]{1,0:T(8,128)(2,1)S(1)} custom-call(bf16[768,384]{1,0:T(8,128)(2,1)S(1)} %bitcast.109, f32[96,2880]{1,0:T(8,128)S(1)} %experts.2.start_ref, bf16[8,540,2880]{2,1,0:T(8,128)(2,1)} %all-gather.4.cloned.1.call-done.weight_ref), custom_call_target="tpu_custom_call" | custom-call | flops 2090188800 | bytes 21772800 | tf_op jit(solution)/shard_map/experts/pallas_call | solution.py:211
  166.6 44.3 %all_to_all.26 = bf16[32,24,384]{2,1,0:T(8,128)(2,1)S(1)} all-to-all(bf16[32,24,384]{2,1,0:T(8,128)(2,1)S(1)} %bitcast.111), channel_id=1, replica_groups=mesh['seq'=32,'exp'=8,'batch'=2] {'seq'}, dimensions={0} | all-to-all | bytes 1179648 | tf_op jit(solution)/shard_map/combine/all_to_all | solution.py:376
  210.8 0.7 combine.1
  211.5 16.7 %all_to_all.27 = bf16[8,16,2880]{2,1,0:T(8,128)(2,1)S(1)} all-to-all(bf16[8,16,2880]{2,1,0:T(8,128)(2,1)S(1)} %bitcast.110), channel_id=1, replica_groups=mesh['seq'=32,'exp'=8,'batch'=2] {'exp'}, dimensions={0} | all-to-all | bytes 1474560 | tf_op jit(solution)/shard_map/combine/all_to_all | solution.py:386
  228.3 0.7 fusion.22
  (61 shorter events, 3.1 us)
Async XLA Ops:
  6.5 61.1 %copy-start = (bf16[256,2880]{0,1:T(8,128)(2,1)S(1)}, bf16[256,2880]{0,1:T(8,128)(2,1)}, u32[]{:S(2)}) copy-start(bf16[256,2880]{0,1:T(8,128)(2,1)} %param.14) | copy-start | bytes 4423684
  6.5 4.0 %copy-start.3 = (bf16[1,128,128]{2,1,0:T(8,128)(2,1)S(1)}, bf16[1,128,128]{2,1,0:T(8,128)(2,1)}, u32[]{:S(2)}) copy-start(bf16[1,128,128]{2,1,0:T(8,128)(2,1)} %param.12) | copy-start | bytes 98308
  6.5 22.2 %copy-start.2 = (bf16[1,128,256]{2,1,0:T(8,128)(2,1)S(1)}, bf16[1,128,256]{2,1,0:T(8,128)(2,1)}, u32[]{:S(2)}) copy-start(bf16[1,128,256]{2,1,0:T(8,128)(2,1)} %param.11) | copy-start | bytes 196612
  6.5 23.5 %copy-start.7 = (bf16[1,128,4]{1,2,0:T(4,128)(2,1)S(1)}, bf16[1,128,4]{1,2,0:T(4,128)(2,1)}, u32[]{:S(2)}) copy-start(bf16[1,128,4]{1,2,0:T(4,128)(2,1)} %param.18) | copy-start | bytes 3076
  6.5 23.5 %copy-start.5 = (s32[1,128,4]{1,2,0:T(4,128)S(1)}, s32[1,128,4]{1,2,0:T(4,128)}, u32[]{:S(2)}) copy-start(s32[1,128,4]{1,2,0:T(4,128)} %param.17) | copy-start | bytes 6148
  6.5 149.7 %all-gather.4.cloned.1.call-start = ((), (), s32[]{:S(2)}) async-start(), calls=%async_computation.5 | async-start | bytes 28827648 | tf_op jit(solution)/shard_map/gather_weights/all_gather | solution.py:263
  11.6 43.4 %all-to-all-start = ((bf16[16,128,128]{1,2,0:T(8,128)(2,1)}), bf16[16,128,128]{1,2,0:T(8,128)(2,1)S(1)}, u32[]{:S(2)}, u32[]{:S(2)}) async-start(bf16[16,128,128]{1,2,0:T(8,128)(2,1)} %broadcast_in_dim.35), calls=%async_computation | async-start | bytes 1048576 | tf_op jit(solution)/shard_map/gather_keys/all_to_all | solution.py:270
  26.8 65.0 %collective-permute-start.4 = (bf16[540,2880]{1,0:T(8,128)(2,1)}, bf16[540,2880]{1,0:T(8,128)(2,1)}, u32[]{:S(2)}, u32[]{:S(2)}) collective-permute-start(bf16[540,2880]{1,0:T(8,128)(2,1)} %gather_weights.1), channel_id=1, source_target_pairs={{0,2},{2,0},{4,6},{6,4},{8,10},{10,8},{12,14},{14,12},{1,3},{3,1},... | collective-permute-start | bytes 9331208 | tf_op jit(solution)/shard_map/gather_weights/ppermute | solution.py:265
  28.7 6.4 %collective-permute-start = (bf16[128,256]{1,0:T(8,128)(2,1)S(1)}, bf16[128,256]{1,0:T(8,128)(2,1)S(1)}, u32[]{:S(2)}, u32[]{:S(2)}) collective-permute-start(bf16[128,256]{1,0:T(8,128)(2,1)S(1)} %bitcast.119), channel_id=1, source_target_pairs={{256,0},{272,16},{288,32},{304,48},{320,64},{336,80},{352,96},{368... | collective-permute-start | bytes 196616 | tf_op jit(solution)/shard_map/gather_keys/ppermute | solution.py:276
  58.4 7.0 %copy-start.6 = (f32[4]{0:T(128)S(1)}, f32[4]{0:T(128)}, u32[]{:S(2)}) copy-start(f32[4]{0:T(128)} %param.13) | copy-start | bytes 52
  58.5 33.1 %copy-start.1 = (bf16[1,16,2880]{2,1,0:T(8,128)(2,1)S(1)}, bf16[1,16,2880]{2,1,0:T(8,128)(2,1)}, u32[]{:S(2)}) copy-start(bf16[1,16,2880]{2,1,0:T(8,128)(2,1)} %param.15) | copy-start | bytes 276484
  58.5 33.2 %copy-start.4 = (f32[2880]{0:T(1024)S(1)}, f32[2880]{0:T(1024)}, u32[]{:S(2)}) copy-start(f32[2880]{0:T(1024)} %param.16) | copy-start | bytes 34564
  58.5 6.9 %collective-permute-start.1 = (f32[2,4,128]{2,1,0:T(4,128)S(1)}, f32[2,4,128]{2,1,0:T(4,128)S(1)}, u32[]{:S(2)}, u32[]{:S(2)}) collective-permute-start(f32[2,4,128]{2,1,0:T(4,128)S(1)} %pad_maximum_fusion), channel_id=1, source_target_pairs={{0,256},{16,272},{32,288},{48,304},{64,320},{80,336},{96,352},{112... | collective-permute-start | bytes 12296 | tf_op jit(solution)/shard_map/attend/ppermute | solution.py:324
  64.1 3.2 %collective-permute-start.2 = (bf16[4,128,64]{1,2,0:T(8,128)(2,1)S(1)}, bf16[4,128,64]{1,2,0:T(8,128)(2,1)S(1)}, u32[]{:S(2)}, u32[]{:S(2)}) collective-permute-start(bf16[4,128,64]{1,2,0:T(8,128)(2,1)S(1)} %slice.90), channel_id=1, source_target_pairs={{0,256},{16,272},{32,288},{48,304},{64,320},{80,336},{96,352},{112... | collective-permute-start | bytes 196616 | tf_op jit(solution)/shard_map/attend/ppermute | solution.py:325
  69.0 3.8 %collective-permute-start.3 = (bf16[4,16,2880]{2,1,0:T(8,128)(2,1)}, bf16[4,16,2880]{2,1,0:T(8,128)(2,1)S(1)}, u32[]{:S(2)}, u32[]{:S(2)}) collective-permute-start(bf16[4,16,2880]{2,1,0:T(8,128)(2,1)} %fusion.9), channel_id=1, source_target_pairs={{0,2},{2,0},{4,6},{6,4},{8,10},{10,8},{12,14},{14,12},{1,3},{3,1},... | collective-permute-start | bytes 1105928 | tf_op jit(solution)/shard_map/project/ppermute | solution.py:346
  73.6 17.8 %all-to-all-start.1 = ((bf16[4,16,2880]{2,1,0:T(8,128)(2,1)}), bf16[4,16,2880]{2,1,0:T(8,128)(2,1)S(1)}, u32[]{:S(2)}, u32[]{:S(2)}) async-start(bf16[4,16,2880]{2,1,0:T(8,128)(2,1)} %fusion.8), calls=%async_computation.1 | async-start | bytes 753664 | tf_op jit(solution)/shard_map/project/all_to_all | solution.py:349
Sparse Core Ops, SparseCore 0:
  10.7 141.0 all-gather.3

commit v5 on v4

--- a/solution.py
+++ b/solution.py
@@ -7,6 +7,7 @@
 
 HEAD = 64
 TILE = 16
+LANES = 128
 CHUNK = 384
 CAP = 24
 GROUP = 24
@@ -15,7 +16,11 @@
 
 
 def pack_kernel(gate_ref, up_ref, down_ref, out_ref):
-    out_ref[...] = jnp.concatenate([gate_ref[...], up_ref[...], down_ref[...]], axis=0)
+    half = up_ref.shape[0] // 2
+    up = up_ref[...]
+    left = jnp.concatenate([gate_ref[...], up[:half]], axis=0)
+    right = jnp.concatenate([up[half:], down_ref[...]], axis=0)
+    out_ref[...] = jnp.concatenate([left, right], axis=1)
 
 
 def pack_weights(gate_across, up_across, down):
@@ -23,7 +28,7 @@
     depth = 3 * units
     return pl.pallas_call(
         pack_kernel,
-        out_shape=jax.ShapeDtypeStruct((depth, width), down.dtype),
+        out_shape=jax.ShapeDtypeStruct((depth // 2, 2 * width), down.dtype),
         compiler_params=pltpu.CompilerParams(vmem_limit_bytes=56 * 1024 * 1024),
         cost_estimate=pl.CostEstimate(
             flops=0, bytes_accessed=4 * depth * width, transcendentals=0
@@ -118,29 +123,38 @@
     )(selector, normed)
 
 
-def group_term(weight_ref, rows_across):
-    units = weight_ref.shape[0] // 3
-    count = rows_across.shape[1]
-    lift_rows = -(-2 * units // TILE) * TILE
-    down_from = 2 * units // TILE * TILE
-    cut = lift_rows // (2 * TILE) * TILE
-    both = jnp.concatenate(
+def pad_across(rows_across):
+    width, count = rows_across.shape
+    spare = jnp.zeros((-width % LANES, count), rows_across.dtype)
+    return (
+        jnp.concatenate([rows_across, spare], axis=0),
+        jnp.concatenate([spare, rows_across], axis=0),
+    )
+
+
+def group_term(weight_ref, across):
+    span, count = across[0].shape
+    units = weight_ref.shape[0] * 2 // 3
+    half = units // 2
+    low = weight_ref.shape[1] - span
+    up_rows = -(-half // TILE) * TILE
+    down_from = half // TILE * TILE
+    cut = units // TILE * TILE
+    left = jnp.concatenate(
         [
-            jnp.dot(weight_ref[:cut, :], rows_across, preferred_element_type=jnp.float32),
-            jnp.dot(
-                weight_ref[cut:lift_rows, :], rows_across, preferred_element_type=jnp.float32
-            ),
+            jnp.dot(weight_ref[:cut, :span], across[0], preferred_element_type=jnp.float32),
+            jnp.dot(weight_ref[cut:, :span], across[0], preferred_element_type=jnp.float32),
         ],
         axis=0,
     )
-    gate = both[:units]
-    lifted = both[units : 2 * units]
+    right = jnp.dot(weight_ref[:up_rows, low:], across[1], preferred_element_type=jnp.float32)
+    gate = left[:units]
+    lifted = jnp.concatenate([left[units:], right[:half]], axis=0)
     hidden = gate * jax.nn.sigmoid(1.702 * gate) * (lifted + 1.0)
-    lead = jnp.zeros((2 * units - down_from, count), jnp.float32)
-    hidden = jnp.concatenate([lead, hidden], axis=0)
+    lead = jnp.zeros((half - down_from, count), jnp.float32)
     return jnp.dot(
-        hidden.T.astype(jnp.bfloat16),
-        weight_ref[down_from:, :],
+        jnp.concatenate([lead, hidden], axis=0).T.astype(jnp.bfloat16),
+        weight_ref[down_from:, low:],
         preferred_element_type=jnp.float32,
     )
 
@@ -150,12 +164,14 @@
     copy = pltpu.make_async_copy(peer_ref, held_ref, sem)
     copy.start()
     rows_across = load_chunks(chunks_ref, count).T[:width].astype(jnp.bfloat16)
+    across = pad_across(rows_across)
     copy.wait()
-    total_ref[...] = group_term(held_ref, rows_across)
+    term = group_term(held_ref, across)
+    total_ref[...] = term[:, term.shape[1] - width :]
 
 
 def run_peer(chunk_rows, peer):
-    depth, width = peer.shape
+    depth, width = peer.shape[0] * 2, peer.shape[1] // 2
     count = chunk_rows.shape[0] // -(-width // CHUNK)
     return pl.pallas_call(
         peer_kernel,
@@ -166,7 +182,7 @@
         out_specs=pl.BlockSpec(memory_space=pltpu.VMEM),
         out_shape=jax.ShapeDtypeStruct((count, width), jnp.float32),
         scratch_shapes=[
-            pltpu.VMEM((depth, width), jnp.bfloat16),
+            pltpu.VMEM(peer.shape, jnp.bfloat16),
             pltpu.SemaphoreType.DMA,
         ],
         compiler_params=pltpu.CompilerParams(vmem_limit_bytes=24 * 1024 * 1024),
@@ -179,7 +195,7 @@
 
 
 def expert_kernel(
-    chunks_ref, start_ref, weight_ref, out_ref, held_ref, total_ref, ready_ref, sems, out_sems
+    chunks_ref, start_ref, weight_ref, out_ref, held_ref, total_ref, wide_ref, sems
 ):
     groups = weight_ref.shape[0]
     others = held_ref.shape[0]
@@ -193,21 +209,24 @@
 
     for i in range(others):
         fetch(i).start()
-    total_ref[...] = start_ref[...]
     rows_across = load_chunks(chunks_ref, count).T[:width].astype(jnp.bfloat16)
+    across = pad_across(rows_across)
     for i in range(others):
         fetch(i).wait()
-        total_ref[...] += group_term(held_ref.at[i], rows_across)
-    store_chunks(total_ref, ready_ref)
-    copy = pltpu.make_async_copy(ready_ref, out_ref, out_sems)
-    copy.start()
-    copy.wait()
+        term = group_term(held_ref.at[i], across)
+        if i == 0:
+            wide_ref[...] = term
+        else:
+            wide_ref[...] += term
+    total_ref[...] = start_ref[...] + wide_ref[:, wide_ref.shape[1] - width :]
+    store_chunks(total_ref, out_ref)
 
 
 def run_expert(chunk_rows, start, weights):
-    groups, depth, width = weights.shape
-    count = start.shape[0]
+    groups, depth, _ = weights.shape
+    count, width = start.shape
     others = groups - 1
+    span = -(-width // LANES) * LANES
     return pl.pallas_call(
         expert_kernel,
         in_specs=[
@@ -215,20 +234,19 @@
             pl.BlockSpec(memory_space=pltpu.VMEM),
             pl.BlockSpec(memory_space=pl.ANY),
         ],
-        out_specs=pl.BlockSpec(memory_space=pltpu.HBM),
+        out_specs=pl.BlockSpec(memory_space=pltpu.VMEM),
         out_shape=jax.ShapeDtypeStruct(chunk_rows.shape, jnp.bfloat16),
         scratch_shapes=[
-            pltpu.VMEM((others, depth, width), jnp.bfloat16),
+            pltpu.VMEM((others,) + weights.shape[1:], jnp.bfloat16),
             pltpu.VMEM((count, width), jnp.float32),
-            pltpu.VMEM(chunk_rows.shape, jnp.bfloat16),
+            pltpu.VMEM((count, span), jnp.float32),
             pltpu.SemaphoreType.DMA((others,)),
-            pltpu.SemaphoreType.DMA,
         ],
         compiler_params=pltpu.CompilerParams(vmem_limit_bytes=44 * 1024 * 1024),
         cost_estimate=pl.CostEstimate(
-            flops=2 * count * width * depth * others,
-            bytes_accessed=others * depth * width * 2,
-            transcendentals=count * depth * others // 3,
+            flops=4 * count * width * depth * others,
+            bytes_accessed=others * depth * width * 4,
+            transcendentals=count * depth * others // 2,
         ),
     )(chunk_rows, start, weights)
 
@@ -300,30 +318,35 @@
         selector, combiner, near = lax.optimization_barrier((selector, combiner, near))
 
     with jax.named_scope("attend"):
-        grid = jnp.concatenate([queries[0], guests], axis=0)
-        grid = grid.reshape(2 * block_rows, heads, HEAD)
         own_pos = (seq_rank % RUN) * block_rows + jnp.arange(block_rows, dtype=jnp.int32)
-        query_pos = jnp.concatenate([own_pos, jnp.full((block_rows,), run_rows, jnp.int32)])
         key_pos = jnp.arange(run_rows, dtype=jnp.int32)
-        scores = (
-            jnp.einsum("igd,jd->gij", grid, near[:, :HEAD], preferred_element_type=jnp.float32)
-            * 0.125
-        )
-        scores = jnp.where(key_pos[None, :] <= query_pos[:, None], scores, -1e30)
-        top = jnp.max(scores, axis=-1)
-        numerators = jnp.exp(scores - top[..., None])
-        sums = jnp.sum(numerators, axis=-1)
-        weighted = jnp.einsum(
-            "gij,jd->gid",
-            numerators.astype(jnp.bfloat16),
-            near[:, HEAD:],
-            preferred_element_type=jnp.float32,
-        )
-        guest_stats = jnp.stack([top[:, block_rows:], sums[:, block_rows:]])
-        guest_mix = weighted[:, block_rows:].astype(jnp.bfloat16)
-        far_stats = lax.ppermute(guest_stats, "seq", to_far)
-        far_mix = lax.ppermute(guest_mix, "seq", to_far)
-        top, sums, weighted = top[:, :block_rows], sums[:, :block_rows], weighted[:, :block_rows]
+
+        def attend(rows, allowed):
+            scores = (
+                jnp.einsum(
+                    "igd,jd->gij",
+                    rows.reshape(block_rows, heads, HEAD),
+                    near[:, :HEAD],
+                    preferred_element_type=jnp.float32,
+                )
+                * 0.125
+            )
+            if allowed is not None:
+                scores = jnp.where(allowed, scores, -1e30)
+            top = jnp.max(scores, axis=-1)
+            numerators = jnp.exp(scores - top[..., None])
+            mix = jnp.einsum(
+                "gij,jd->gid",
+                numerators.astype(jnp.bfloat16),
+                near[:, HEAD:],
+                preferred_element_type=jnp.float32,
+            )
+            return top, jnp.sum(numerators, axis=-1), mix
+
+        guest_top, guest_sum, guest_mix = attend(guests, None)
+        far_mix = lax.ppermute(guest_mix.astype(jnp.bfloat16), "seq", to_far)
+        far_stats = lax.ppermute(jnp.stack([guest_top, guest_sum]), "seq", to_far)
+        top, sums, weighted = attend(queries[0], key_pos[None, :] <= own_pos[:, None])
         far_top = jnp.where(seq_rank >= RUN, far_stats[0], -1e30)
         largest = jnp.maximum(jnp.maximum(top, far_top), sinks[:, None])
         near_scale = jnp.exp(top - largest)

time: 236 us -> 233 us (0.987)
  no operation moved by 1% of the time
where the time goes in v5:
time: 233 us
  blocking collectives  122 us (52%)
  waiting for transfers between devices  37.5 us (16%)
  starting transfers between devices  29.5 us (13%)
  Pallas kernels  18.4 us (8%)
  between operations  13.9 us (6%)
  local copies, waits for them, and re-layouts  4.09 us (2%)
  other arithmetic  3.85 us (2%)
  matrix products  3.82 us (2%)
    all_to_all x1, blocking collectives, on_device(): lax.all_to_all(done.reshape(seq_devices, chunks * share, CHUNK), 'seq', s...  44.5 us
    all_to_all x1, blocking collectives, on_device(): lax.all_to_all(outgoing, 'seq', split_axis=0, concat_axis=0, tiled=True)  44.2 us
    all_to_all x1, waiting for transfers between devices, on_device(): lax.all_to_all(copies, 'seq', split_axis=0, concat_axis=0, tiled=True, ax...  19.8 us
    all_to_all x1, blocking collectives, on_device(): lax.all_to_all(term.reshape(exp_devices, own_rows, width), 'exp', split_a...  16.7 us
    all_to_all x1, starting transfers between devices, on_device(): lax.all_to_all(copies, 'seq', split_axis=0, concat_axis=0, tiled=True, ax...  15.2 us
    all_gather x1, blocking collectives, on_device(): lax.all_gather(normed_own, 'exp', axis=0, tiled=True, axis_index_groups=c...  14.3 us
    all_to_all x1, waiting for transfers between devices, on_device(): lax.all_to_all(pair, 'exp', split_axis=0, concat_axis=0, tiled=True, axis...  12.8 us
    pallas_call x1, Pallas kernels, run_expert(): pl.pallas_call(expert_kernel, in_specs=[pl.BlockSpec(memory_space=pltpu.V...  9.46 us
  transfers between devices with their start and end apart: 8, of which 5 were waited for; matrix products, arithmetic and copies ran while one was open for 5% of the time, Pallas kernels for 2%

profile of v5, /device:TPU:32, one launch (start us, length us, event | category | flops | bytes accessed | tf_op | source)
XLA Modules:
  0.0 233.0 jit_solution(7717486508625279086)
XLA Ops:
  6.6 4.3 %gather_weights.1 = bf16[270,5760]{1,0:T(8,128)(2,1)} custom-call(bf16[180,2880]{1,0:T(8,128)(2,1)} %bitcast.136, bf16[180,2880]{1,0:T(8,128)(2,1)} %bitcast.137, bf16[180,2880]{1,0:T(8,128)(2,1)} %bitcast.138), custom_call_target="tpu_custom_call" | custom-call | bytes 6220800 | tf_op jit(solution)/shard_map/gather_weights/pallas_call | solution.py:29
  11.0 0.9 broadcast_in_dim.35
  11.9 15.2 %all-to-all-start = ((bf16[16,128,128]{1,2,0:T(8,128)(2,1)}), bf16[16,128,128]{1,2,0:T(8,128)(2,1)S(1)}, u32[]{:S(2)}, u32[]{:S(2)}) async-start(bf16[16,128,128]{1,2,0:T(8,128)(2,1)} %broadcast_in_dim.35), calls=%async_computation | async-start | bytes 1048576 | tf_op jit(solution)/shard_map/gather_keys/all_to_all | solution.py:288
  27.2 1.9 collective-permute-start.4
  29.1 1.3 collective-permute-start
  33.0 2.5 %collective-permute-done = bf16[128,256]{1,0:T(8,128)(2,1)S(1)} collective-permute-done((bf16[128,256]{1,0:T(8,128)(2,1)S(1)}, bf16[128,256]{1,0:T(8,128)(2,1)S(1)}, u32[]{:S(2)}, u32[]{:S(2)}) %collective-permute-start) | collective-permute-done | bytes 65568 | tf_op jit(solution)/shard_map/gather_keys/ppermute | solution.py:294
  35.6 19.8 %all-to-all-done = bf16[16,128,128]{1,2,0:T(8,128)(2,1)S(1)} async-done(((bf16[16,128,128]{1,2,0:T(8,128)(2,1)}), bf16[16,128,128]{1,2,0:T(8,128)(2,1)S(1)}, u32[]{:S(2)}, u32[]{:S(2)}) %all-to-all-start) | async-done | bytes 524320 | tf_op jit(solution)/shard_map/gather_keys/all_to_all | solution.py:288
  55.5 0.8 bitcast_reduce_fusion
  56.2 0.7 fusion.4
  56.9 3.4 %collective-permute-start.1 = (f32[2,4,128]{2,1,0:T(4,128)S(1)}, f32[2,4,128]{2,1,0:T(4,128)S(1)}, u32[]{:S(2)}, u32[]{:S(2)}) collective-permute-start(f32[2,4,128]{2,1,0:T(4,128)S(1)} %pad_maximum_fusion), channel_id=1, source_target_pairs={{0,256},{16,272},{32,288},{48,304},{64,320},{80,336},{96,352},{112... | collective-permute-start | bytes 12296 | tf_op jit(solution)/shard_map/attend/ppermute | solution.py:348
  60.3 0.8 fusion.15
  61.1 1.3 collective-permute-start.2
  62.5 0.7 fusion.52
  63.2 0.6 fusion.1
  64.3 0.8 fusion.41
  65.4 0.6 fusion.10
  66.0 0.8 fusion.19
  66.8 1.9 collective-permute-start.3
  68.8 1.9 collective-permute-done.3
  70.6 0.8 fusion.18
  71.4 4.5 %all-to-all-start.1 = ((bf16[4,16,2880]{2,1,0:T(8,128)(2,1)}), bf16[4,16,2880]{2,1,0:T(8,128)(2,1)S(1)}, u32[]{:S(2)}, u32[]{:S(2)}) async-start(bf16[4,16,2880]{2,1,0:T(8,128)(2,1)} %fusion.18), calls=%async_computation.1 | async-start | bytes 753664 | tf_op jit(solution)/shard_map/project/all_to_all | solution.py:372
  76.0 12.8 %all-to-all-done.1 = bf16[4,16,2880]{2,1,0:T(8,128)(2,1)S(1)} async-done(((bf16[4,16,2880]{2,1,0:T(8,128)(2,1)}), bf16[4,16,2880]{2,1,0:T(8,128)(2,1)S(1)}, u32[]{:S(2)}, u32[]{:S(2)}) %all-to-all-start.1) | async-done | bytes 368672 | tf_op jit(solution)/shard_map/project/all_to_all | solution.py:372
  89.2 14.3 %all_gather.12 = bf16[64,2880]{1,0:T(8,128)(2,1)S(1)} all-gather(bf16[16,2880]{1,0:T(8,128)(2,1)S(1)} %fusion.35), channel_id=1, replica_groups={{0,4,8,12},{2,6,10,14},{1,5,9,13},{3,7,11,15},{16,20,24,28},{18,22,26,3..., dimensions={0}, use_global_device_ids=true | all-gather | bytes 460800 | tf_op jit(solution)/shard_map/norm/all_gather | solution.py:383
  103.5 2.3 %all_gather.13.normed_ref = bf16[128,2880]{1,0:T(8,128)(2,1)S(1)} all-gather(bf16[64,2880]{1,0:T(8,128)(2,1)S(1)} %all_gather.12), channel_id=1, replica_groups={{0,2},{4,6},{8,10},{12,14},{1,3},{5,7},{9,11},{13,15},{16,18},{20,22},{..., dimensions={0}, use_global_device_ids=true | all-gather | bytes 1105920 | tf_op jit(solution)/shard_map/norm/all_gather | solution.py:387
  105.8 0.7 dispatch.1
  106.5 44.2 %all_to_all.25 = bf16[32,24,384]{2,1,0:T(8,128)(2,1)S(1)} all-to-all(bf16[32,24,384]{2,1,0:T(8,128)(2,1)S(1)} %bitcast.133), channel_id=1, replica_groups=mesh['seq'=32,'exp'=8,'batch'=2] {'seq'}, dimensions={0} | all-to-all | bytes 1179648 | tf_op jit(solution)/shard_map/dispatch/all_to_all | solution.py:391
  150.7 3.3 %experts.2.start_ref = f32[96,2880]{1,0:T(8,128)S(1)} custom-call(bf16[768,384]{1,0:T(8,128)(2,1)S(1)} %bitcast.129, bf16[270,5760]{1,0:T(8,128)(2,1)} %collective-permute-done.4.peer_ref), custom_call_target="tpu_custom_call" | custom-call | flops 298598400 | bytes 3110400 | tf_op jit(solution)/shard_map/experts/pallas_call | solution.py:176
  154.1 9.5 %experts.3 = bf16[768,384]{1,0:T(8,128)(2,1)S(1)} custom-call(bf16[768,384]{1,0:T(8,128)(2,1)S(1)} %bitcast.130, f32[96,2880]{1,0:T(8,128)S(1)} %experts.2.start_ref, bf16[8,270,5760]{2,1,0:T(8,128)(2,1)} %all-gather.4.cloned.1.call-done.weight_ref), custom_call_target="tpu_custom_call" | custom-call | flops 2090188800 | bytes 21772800 | tf_op jit(solution)/shard_map/experts/pallas_call | solution.py:230
  163.5 44.5 %all_to_all.26 = bf16[32,24,384]{2,1,0:T(8,128)(2,1)S(1)} all-to-all(bf16[32,24,384]{2,1,0:T(8,128)(2,1)S(1)} %bitcast.132), channel_id=1, replica_groups=mesh['seq'=32,'exp'=8,'batch'=2] {'seq'}, dimensions={0} | all-to-all | bytes 1179648 | tf_op jit(solution)/shard_map/combine/all_to_all | solution.py:399
  208.0 0.7 combine.1
  208.7 16.7 %all_to_all.27 = bf16[8,16,2880]{2,1,0:T(8,128)(2,1)S(1)} all-to-all(bf16[8,16,2880]{2,1,0:T(8,128)(2,1)S(1)} %bitcast.131), channel_id=1, replica_groups=mesh['seq'=32,'exp'=8,'batch'=2] {'exp'}, dimensions={0} | all-to-all | bytes 1474560 | tf_op jit(solution)/shard_map/combine/all_to_all | solution.py:409
  225.4 0.7 fusion.36
  (59 shorter events, 4.1 us)
Async XLA Ops:
  6.5 58.9 %copy-start = (bf16[256,2880]{0,1:T(8,128)(2,1)S(1)}, bf16[256,2880]{0,1:T(8,128)(2,1)}, u32[]{:S(2)}) copy-start(bf16[256,2880]{0,1:T(8,128)(2,1)} %param.14) | copy-start | bytes 4423684
  6.5 147.5 %all-gather.4.cloned.1.call-start = ((), (), s32[]{:S(2)}) async-start(), calls=%async_computation.5 | async-start | bytes 28200960 | tf_op jit(solution)/shard_map/gather_weights/all_gather | solution.py:281
  6.5 4.4 %copy-start.3 = (bf16[1,128,128]{2,1,0:T(8,128)(2,1)S(1)}, bf16[1,128,128]{2,1,0:T(8,128)(2,1)}, u32[]{:S(2)}) copy-start(bf16[1,128,128]{2,1,0:T(8,128)(2,1)} %param.12) | copy-start | bytes 98308
  6.5 22.5 %copy-start.2 = (bf16[1,128,256]{2,1,0:T(8,128)(2,1)S(1)}, bf16[1,128,256]{2,1,0:T(8,128)(2,1)}, u32[]{:S(2)}) copy-start(bf16[1,128,256]{2,1,0:T(8,128)(2,1)} %param.11) | copy-start | bytes 196612
  6.5 23.8 %copy-start.6 = (bf16[1,128,4]{1,2,0:T(4,128)(2,1)S(1)}, bf16[1,128,4]{1,2,0:T(4,128)(2,1)}, u32[]{:S(2)}) copy-start(bf16[1,128,4]{1,2,0:T(4,128)(2,1)} %param.18) | copy-start | bytes 3076
  6.6 23.9 %copy-start.5 = (s32[1,128,4]{1,2,0:T(4,128)S(1)}, s32[1,128,4]{1,2,0:T(4,128)}, u32[]{:S(2)}) copy-start(s32[1,128,4]{1,2,0:T(4,128)} %param.17) | copy-start | bytes 6148
  11.9 43.4 %all-to-all-start = ((bf16[16,128,128]{1,2,0:T(8,128)(2,1)}), bf16[16,128,128]{1,2,0:T(8,128)(2,1)S(1)}, u32[]{:S(2)}, u32[]{:S(2)}) async-start(bf16[16,128,128]{1,2,0:T(8,128)(2,1)} %broadcast_in_dim.35), calls=%async_computation | async-start | bytes 1048576 | tf_op jit(solution)/shard_map/gather_keys/all_to_all | solution.py:288
  27.2 62.0 %collective-permute-start.4 = (bf16[270,5760]{1,0:T(8,128)(2,1)}, bf16[270,5760]{1,0:T(8,128)(2,1)}, u32[]{:S(2)}, u32[]{:S(2)}) collective-permute-start(bf16[270,5760]{1,0:T(8,128)(2,1)} %gather_weights.1), channel_id=1, source_target_pairs={{0,2},{2,0},{4,6},{6,4},{8,10},{10,8},{12,14},{14,12},{1,3},{3,1},... | collective-permute-start | bytes 9331208 | tf_op jit(solution)/shard_map/gather_weights/ppermute | solution.py:283
  29.1 6.4 %collective-permute-start = (bf16[128,256]{1,0:T(8,128)(2,1)S(1)}, bf16[128,256]{1,0:T(8,128)(2,1)S(1)}, u32[]{:S(2)}, u32[]{:S(2)}) collective-permute-start(bf16[128,256]{1,0:T(8,128)(2,1)S(1)} %bitcast.141), channel_id=1, source_target_pairs={{256,0},{272,16},{288,32},{304,48},{320,64},{336,80},{352,96},{368... | collective-permute-start | bytes 196616 | tf_op jit(solution)/shard_map/gather_keys/ppermute | solution.py:294
  56.9 6.9 %collective-permute-start.1 = (f32[2,4,128]{2,1,0:T(4,128)S(1)}, f32[2,4,128]{2,1,0:T(4,128)S(1)}, u32[]{:S(2)}, u32[]{:S(2)}) collective-permute-start(f32[2,4,128]{2,1,0:T(4,128)S(1)} %pad_maximum_fusion), channel_id=1, source_target_pairs={{0,256},{16,272},{32,288},{48,304},{64,320},{80,336},{96,352},{112... | collective-permute-start | bytes 12296 | tf_op jit(solution)/shard_map/attend/ppermute | solution.py:348
  61.1 3.2 %collective-permute-start.2 = (bf16[4,128,64]{1,2,0:T(8,128)(2,1)S(1)}, bf16[4,128,64]{1,2,0:T(8,128)(2,1)S(1)}, u32[]{:S(2)}, u32[]{:S(2)}) collective-permute-start(bf16[4,128,64]{1,2,0:T(8,128)(2,1)S(1)} %fusion.15), channel_id=1, source_target_pairs={{0,256},{16,272},{32,288},{48,304},{64,320},{80,336},{96,352},{112... | collective-permute-start | bytes 196616 | tf_op jit(solution)/shard_map/attend/ppermute | solution.py:347
  62.4 1.4 copy-start.7
  65.1 23.8 %copy-start.1 = (bf16[1,16,2880]{2,1,0:T(8,128)(2,1)S(1)}, bf16[1,16,2880]{2,1,0:T(8,128)(2,1)}, u32[]{:S(2)}) copy-start(bf16[1,16,2880]{2,1,0:T(8,128)(2,1)} %param.15) | copy-start | bytes 276484
  65.1 24.0 %copy-start.4 = (f32[2880]{0:T(1024)S(1)}, f32[2880]{0:T(1024)}, u32[]{:S(2)}) copy-start(f32[2880]{0:T(1024)} %param.16) | copy-start | bytes 34564
  66.8 3.8 %collective-permute-start.3 = (bf16[4,16,2880]{2,1,0:T(8,128)(2,1)}, bf16[4,16,2880]{2,1,0:T(8,128)(2,1)S(1)}, u32[]{:S(2)}, u32[]{:S(2)}) collective-permute-start(bf16[4,16,2880]{2,1,0:T(8,128)(2,1)} %fusion.19), channel_id=1, source_target_pairs={{0,2},{2,0},{4,6},{6,4},{8,10},{10,8},{12,14},{14,12},{1,3},{3,1},... | collective-permute-start | bytes 1105928 | tf_op jit(solution)/shard_map/project/ppermute | solution.py:369
  71.4 17.4 %all-to-all-start.1 = ((bf16[4,16,2880]{2,1,0:T(8,128)(2,1)}), bf16[4,16,2880]{2,1,0:T(8,128)(2,1)S(1)}, u32[]{:S(2)}, u32[]{:S(2)}) async-start(bf16[4,16,2880]{2,1,0:T(8,128)(2,1)} %fusion.18), calls=%async_computation.1 | async-start | bytes 753664 | tf_op jit(solution)/shard_map/project/all_to_all | solution.py:372
Sparse Core Ops, SparseCore 0:
  11.0 138.6 all-gather.3

commit v6 on v5

--- a/solution.py
+++ b/solution.py
@@ -15,23 +15,52 @@
 RUN = 16
 
 
-def pack_kernel(gate_ref, up_ref, down_ref, out_ref):
+def pack_kernel(
+    gate_ref, up_ref, down_ref, out_ref, gate_vmem, up_vmem, down_vmem, packed_ref, sems, out_sems
+):
+    width = gate_ref.shape[1]
     half = up_ref.shape[0] // 2
-    up = up_ref[...]
-    left = jnp.concatenate([gate_ref[...], up[:half]], axis=0)
-    right = jnp.concatenate([up[half:], down_ref[...]], axis=0)
-    out_ref[...] = jnp.concatenate([left, right], axis=1)
+    low = width // LANES * LANES
+    pairs = ((gate_ref, gate_vmem), (up_ref, up_vmem), (down_ref, down_vmem))
+    loads = [pltpu.make_async_copy(s, d, sems.at[i]) for i, (s, d) in enumerate(pairs)]
+    spans = (slice(0, low), slice(low, 2 * width))
+    stores = [
+        pltpu.make_async_copy(packed_ref.at[:, span], out_ref.at[:, span], out_sems.at[i])
+        for i, span in enumerate(spans)
+    ]
+    for load in loads:
+        load.start()
+    loads[0].wait()
+    loads[1].wait()
+    up = up_vmem[...]
+    left = jnp.concatenate([gate_vmem[...], up[:half]], axis=0)
+    packed_ref[:, :low] = left[:, :low]
+    stores[0].start()
+    loads[2].wait()
+    right = jnp.concatenate([up[half:], down_vmem[...]], axis=0)
+    packed_ref[:, low:] = jnp.concatenate([left[:, low:], right], axis=1)
+    stores[1].start()
+    for store in stores:
+        store.wait()
 
 
 def pack_weights(gate_across, up_across, down):
     units, width = down.shape
-    depth = 3 * units
+    packed = (3 * units // 2, 2 * width)
     return pl.pallas_call(
         pack_kernel,
-        out_shape=jax.ShapeDtypeStruct((depth // 2, 2 * width), down.dtype),
+        in_specs=[pl.BlockSpec(memory_space=pl.ANY)] * 3,
+        out_specs=pl.BlockSpec(memory_space=pl.ANY),
+        out_shape=jax.ShapeDtypeStruct(packed, down.dtype),
+        scratch_shapes=[pltpu.VMEM(down.shape, down.dtype)] * 3
+        + [
+            pltpu.VMEM(packed, down.dtype),
+            pltpu.SemaphoreType.DMA((3,)),
+            pltpu.SemaphoreType.DMA((2,)),
+        ],
         compiler_params=pltpu.CompilerParams(vmem_limit_bytes=56 * 1024 * 1024),
         cost_estimate=pl.CostEstimate(
-            flops=0, bytes_accessed=4 * depth * width, transcendentals=0
+            flops=0, bytes_accessed=12 * units * width, transcendentals=0
         ),
     )(gate_across, up_across, down)
 

time: 233 us -> 233 us (level)
  no operation moved by 1% of the time
where the time goes in v6:
time: 233 us; the launch traced here: 232 us
  blocking collectives  122 us (52%)
  waiting for transfers between devices  37.5 us (16%)
  starting transfers between devices  29.5 us (13%)
  Pallas kernels  17.9 us (8%)
  between operations  13.9 us (6%)
  local copies, waits for them, and re-layouts  4.09 us (2%)
  other arithmetic  3.85 us (2%)
  matrix products  3.81 us (2%)
    all_to_all x1, blocking collectives, on_device(): lax.all_to_all(done.reshape(seq_devices, chunks * share, CHUNK), 'seq', s...  44.4 us
    all_to_all x1, blocking collectives, on_device(): lax.all_to_all(outgoing, 'seq', split_axis=0, concat_axis=0, tiled=True)  44.2 us
    all_to_all x1, waiting for transfers between devices, on_device(): lax.all_to_all(copies, 'seq', split_axis=0, concat_axis=0, tiled=True, ax...  19.8 us
    all_to_all x1, blocking collectives, on_device(): lax.all_to_all(term.reshape(exp_devices, own_rows, width), 'exp', split_a...  16.7 us
    all_to_all x1, starting transfers between devices, on_device(): lax.all_to_all(copies, 'seq', split_axis=0, concat_axis=0, tiled=True, ax...  15.2 us
    all_gather x1, blocking collectives, on_device(): lax.all_gather(normed_own, 'exp', axis=0, tiled=True, axis_index_groups=c...  14.3 us
    all_to_all x1, waiting for transfers between devices, on_device(): lax.all_to_all(pair, 'exp', split_axis=0, concat_axis=0, tiled=True, axis...  12.8 us
    pallas_call x1, Pallas kernels, run_expert(): pl.pallas_call(expert_kernel, in_specs=[pl.BlockSpec(memory_space=pltpu.V...  9.44 us
  transfers between devices with their start and end apart: 8, of which 5 were waited for; matrix products, arithmetic and copies ran while one was open for 5% of the time, Pallas kernels for 2%

profile of v6, /device:TPU:32, one launch (start us, length us, event | category | flops | bytes accessed | tf_op | source)
XLA Modules:
  0.0 232.5 jit_solution(2473318323430881027)
XLA Ops:
  6.6 3.8 %gather_weights.1 = bf16[270,5760]{1,0:T(8,128)(2,1)} custom-call(bf16[180,2880]{1,0:T(8,128)(2,1)} %bitcast.136, bf16[180,2880]{1,0:T(8,128)(2,1)} %bitcast.137, bf16[180,2880]{1,0:T(8,128)(2,1)} %bitcast.138), custom_call_target="tpu_custom_call" | custom-call | bytes 6220800 | tf_op jit(solution)/shard_map/gather_weights/pallas_call | solution.py:50
  10.5 0.9 broadcast_in_dim.35
  11.4 15.2 %all-to-all-start = ((bf16[16,128,128]{1,2,0:T(8,128)(2,1)}), bf16[16,128,128]{1,2,0:T(8,128)(2,1)S(1)}, u32[]{:S(2)}, u32[]{:S(2)}) async-start(bf16[16,128,128]{1,2,0:T(8,128)(2,1)} %broadcast_in_dim.35), calls=%async_computation | async-start | bytes 1048576 | tf_op jit(solution)/shard_map/gather_keys/all_to_all | solution.py:317
  26.7 1.9 collective-permute-start.4
  28.6 1.3 collective-permute-start
  32.5 2.5 %collective-permute-done = bf16[128,256]{1,0:T(8,128)(2,1)S(1)} collective-permute-done((bf16[128,256]{1,0:T(8,128)(2,1)S(1)}, bf16[128,256]{1,0:T(8,128)(2,1)S(1)}, u32[]{:S(2)}, u32[]{:S(2)}) %collective-permute-start) | collective-permute-done | bytes 65568 | tf_op jit(solution)/shard_map/gather_keys/ppermute | solution.py:323
  35.1 19.8 %all-to-all-done = bf16[16,128,128]{1,2,0:T(8,128)(2,1)S(1)} async-done(((bf16[16,128,128]{1,2,0:T(8,128)(2,1)}), bf16[16,128,128]{1,2,0:T(8,128)(2,1)S(1)}, u32[]{:S(2)}, u32[]{:S(2)}) %all-to-all-start) | async-done | bytes 524320 | tf_op jit(solution)/shard_map/gather_keys/all_to_all | solution.py:317
  55.0 0.7 bitcast_reduce_fusion
  55.7 0.7 fusion.4
  56.4 3.4 %collective-permute-start.1 = (f32[2,4,128]{2,1,0:T(4,128)S(1)}, f32[2,4,128]{2,1,0:T(4,128)S(1)}, u32[]{:S(2)}, u32[]{:S(2)}) collective-permute-start(f32[2,4,128]{2,1,0:T(4,128)S(1)} %pad_maximum_fusion), channel_id=1, source_target_pairs={{0,256},{16,272},{32,288},{48,304},{64,320},{80,336},{96,352},{112... | collective-permute-start | bytes 12296 | tf_op jit(solution)/shard_map/attend/ppermute | solution.py:377
  59.8 0.8 fusion.15
  60.6 1.3 collective-permute-start.2
  62.0 0.7 fusion.52
  62.7 0.6 fusion.1
  63.8 0.8 fusion.41
  64.9 0.6 fusion.10
  65.6 0.8 fusion.19
  66.3 1.9 collective-permute-start.3
  68.3 1.9 collective-permute-done.3
  70.1 0.8 fusion.18
  70.9 4.5 %all-to-all-start.1 = ((bf16[4,16,2880]{2,1,0:T(8,128)(2,1)}), bf16[4,16,2880]{2,1,0:T(8,128)(2,1)S(1)}, u32[]{:S(2)}, u32[]{:S(2)}) async-start(bf16[4,16,2880]{2,1,0:T(8,128)(2,1)} %fusion.18), calls=%async_computation.1 | async-start | bytes 753664 | tf_op jit(solution)/shard_map/project/all_to_all | solution.py:401
  75.5 12.8 %all-to-all-done.1 = bf16[4,16,2880]{2,1,0:T(8,128)(2,1)S(1)} async-done(((bf16[4,16,2880]{2,1,0:T(8,128)(2,1)}), bf16[4,16,2880]{2,1,0:T(8,128)(2,1)S(1)}, u32[]{:S(2)}, u32[]{:S(2)}) %all-to-all-start.1) | async-done | bytes 368672 | tf_op jit(solution)/shard_map/project/all_to_all | solution.py:401
  88.7 14.3 %all_gather.12 = bf16[64,2880]{1,0:T(8,128)(2,1)S(1)} all-gather(bf16[16,2880]{1,0:T(8,128)(2,1)S(1)} %fusion.35), channel_id=1, replica_groups={{0,4,8,12},{2,6,10,14},{1,5,9,13},{3,7,11,15},{16,20,24,28},{18,22,26,3..., dimensions={0}, use_global_device_ids=true | all-gather | bytes 460800 | tf_op jit(solution)/shard_map/norm/all_gather | solution.py:412
  103.0 2.3 %all_gather.13.normed_ref = bf16[128,2880]{1,0:T(8,128)(2,1)S(1)} all-gather(bf16[64,2880]{1,0:T(8,128)(2,1)S(1)} %all_gather.12), channel_id=1, replica_groups={{0,2},{4,6},{8,10},{12,14},{1,3},{5,7},{9,11},{13,15},{16,18},{20,22},{..., dimensions={0}, use_global_device_ids=true | all-gather | bytes 1105920 | tf_op jit(solution)/shard_map/norm/all_gather | solution.py:416
  105.3 0.7 dispatch.1
  106.0 44.2 %all_to_all.25 = bf16[32,24,384]{2,1,0:T(8,128)(2,1)S(1)} all-to-all(bf16[32,24,384]{2,1,0:T(8,128)(2,1)S(1)} %bitcast.133), channel_id=1, replica_groups=mesh['seq'=32,'exp'=8,'batch'=2] {'seq'}, dimensions={0} | all-to-all | bytes 1179648 | tf_op jit(solution)/shard_map/dispatch/all_to_all | solution.py:420
  150.2 3.4 %experts.2.start_ref = f32[96,2880]{1,0:T(8,128)S(1)} custom-call(bf16[768,384]{1,0:T(8,128)(2,1)S(1)} %bitcast.129, bf16[270,5760]{1,0:T(8,128)(2,1)} %collective-permute-done.4.peer_ref), custom_call_target="tpu_custom_call" | custom-call | flops 298598400 | bytes 3110400 | tf_op jit(solution)/shard_map/experts/pallas_call | solution.py:205
  153.6 9.4 %experts.3 = bf16[768,384]{1,0:T(8,128)(2,1)S(1)} custom-call(bf16[768,384]{1,0:T(8,128)(2,1)S(1)} %bitcast.130, f32[96,2880]{1,0:T(8,128)S(1)} %experts.2.start_ref, bf16[8,270,5760]{2,1,0:T(8,128)(2,1)} %all-gather.4.cloned.1.call-done.weight_ref), custom_call_target="tpu_custom_call" | custom-call | flops 2090188800 | bytes 21772800 | tf_op jit(solution)/shard_map/experts/pallas_call | solution.py:259
  163.1 44.4 %all_to_all.26 = bf16[32,24,384]{2,1,0:T(8,128)(2,1)S(1)} all-to-all(bf16[32,24,384]{2,1,0:T(8,128)(2,1)S(1)} %bitcast.132), channel_id=1, replica_groups=mesh['seq'=32,'exp'=8,'batch'=2] {'seq'}, dimensions={0} | all-to-all | bytes 1179648 | tf_op jit(solution)/shard_map/combine/all_to_all | solution.py:428
  207.5 0.7 combine.1
  208.2 16.7 %all_to_all.27 = bf16[8,16,2880]{2,1,0:T(8,128)(2,1)S(1)} all-to-all(bf16[8,16,2880]{2,1,0:T(8,128)(2,1)S(1)} %bitcast.131), channel_id=1, replica_groups=mesh['seq'=32,'exp'=8,'batch'=2] {'exp'}, dimensions={0} | all-to-all | bytes 1474560 | tf_op jit(solution)/shard_map/combine/all_to_all | solution.py:438
  225.0 0.7 fusion.36
  (59 shorter events, 4.1 us)
Async XLA Ops:
  6.5 58.4 %copy-start = (bf16[256,2880]{0,1:T(8,128)(2,1)S(1)}, bf16[256,2880]{0,1:T(8,128)(2,1)}, u32[]{:S(2)}) copy-start(bf16[256,2880]{0,1:T(8,128)(2,1)} %param.14) | copy-start | bytes 4423684
  6.5 147.1 %all-gather.4.cloned.1.call-start = ((), (), s32[]{:S(2)}) async-start(), calls=%async_computation.5 | async-start | bytes 28200960 | tf_op jit(solution)/shard_map/gather_weights/all_gather | solution.py:310
  6.5 3.9 %copy-start.3 = (bf16[1,128,128]{2,1,0:T(8,128)(2,1)S(1)}, bf16[1,128,128]{2,1,0:T(8,128)(2,1)}, u32[]{:S(2)}) copy-start(bf16[1,128,128]{2,1,0:T(8,128)(2,1)} %param.12) | copy-start | bytes 98308
  6.5 22.0 %copy-start.2 = (bf16[1,128,256]{2,1,0:T(8,128)(2,1)S(1)}, bf16[1,128,256]{2,1,0:T(8,128)(2,1)}, u32[]{:S(2)}) copy-start(bf16[1,128,256]{2,1,0:T(8,128)(2,1)} %param.11) | copy-start | bytes 196612
  6.5 23.3 %copy-start.6 = (bf16[1,128,4]{1,2,0:T(4,128)(2,1)S(1)}, bf16[1,128,4]{1,2,0:T(4,128)(2,1)}, u32[]{:S(2)}) copy-start(bf16[1,128,4]{1,2,0:T(4,128)(2,1)} %param.18) | copy-start | bytes 3076
  6.6 23.4 %copy-start.5 = (s32[1,128,4]{1,2,0:T(4,128)S(1)}, s32[1,128,4]{1,2,0:T(4,128)}, u32[]{:S(2)}) copy-start(s32[1,128,4]{1,2,0:T(4,128)} %param.17) | copy-start | bytes 6148
  11.4 43.4 %all-to-all-start = ((bf16[16,128,128]{1,2,0:T(8,128)(2,1)}), bf16[16,128,128]{1,2,0:T(8,128)(2,1)S(1)}, u32[]{:S(2)}, u32[]{:S(2)}) async-start(bf16[16,128,128]{1,2,0:T(8,128)(2,1)} %broadcast_in_dim.35), calls=%async_computation | async-start | bytes 1048576 | tf_op jit(solution)/shard_map/gather_keys/all_to_all | solution.py:317
  26.7 62.0 %collective-permute-start.4 = (bf16[270,5760]{1,0:T(8,128)(2,1)}, bf16[270,5760]{1,0:T(8,128)(2,1)}, u32[]{:S(2)}, u32[]{:S(2)}) collective-permute-start(bf16[270,5760]{1,0:T(8,128)(2,1)} %gather_weights.1), channel_id=1, source_target_pairs={{0,2},{2,0},{4,6},{6,4},{8,10},{10,8},{12,14},{14,12},{1,3},{3,1},... | collective-permute-start | bytes 9331208 | tf_op jit(solution)/shard_map/gather_weights/ppermute | solution.py:312
  28.6 6.4 %collective-permute-start = (bf16[128,256]{1,0:T(8,128)(2,1)S(1)}, bf16[128,256]{1,0:T(8,128)(2,1)S(1)}, u32[]{:S(2)}, u32[]{:S(2)}) collective-permute-start(bf16[128,256]{1,0:T(8,128)(2,1)S(1)} %bitcast.141), channel_id=1, source_target_pairs={{256,0},{272,16},{288,32},{304,48},{320,64},{336,80},{352,96},{368... | collective-permute-start | bytes 196616 | tf_op jit(solution)/shard_map/gather_keys/ppermute | solution.py:323
  56.4 6.9 %collective-permute-start.1 = (f32[2,4,128]{2,1,0:T(4,128)S(1)}, f32[2,4,128]{2,1,0:T(4,128)S(1)}, u32[]{:S(2)}, u32[]{:S(2)}) collective-permute-start(f32[2,4,128]{2,1,0:T(4,128)S(1)} %pad_maximum_fusion), channel_id=1, source_target_pairs={{0,256},{16,272},{32,288},{48,304},{64,320},{80,336},{96,352},{112... | collective-permute-start | bytes 12296 | tf_op jit(solution)/shard_map/attend/ppermute | solution.py:377
  60.6 3.2 %collective-permute-start.2 = (bf16[4,128,64]{1,2,0:T(8,128)(2,1)S(1)}, bf16[4,128,64]{1,2,0:T(8,128)(2,1)S(1)}, u32[]{:S(2)}, u32[]{:S(2)}) collective-permute-start(bf16[4,128,64]{1,2,0:T(8,128)(2,1)S(1)} %fusion.15), channel_id=1, source_target_pairs={{0,256},{16,272},{32,288},{48,304},{64,320},{80,336},{96,352},{112... | collective-permute-start | bytes 196616 | tf_op jit(solution)/shard_map/attend/ppermute | solution.py:376
  62.0 1.4 copy-start.7
  64.6 23.8 %copy-start.1 = (bf16[1,16,2880]{2,1,0:T(8,128)(2,1)S(1)}, bf16[1,16,2880]{2,1,0:T(8,128)(2,1)}, u32[]{:S(2)}) copy-start(bf16[1,16,2880]{2,1,0:T(8,128)(2,1)} %param.15) | copy-start | bytes 276484
  64.6 23.9 %copy-start.4 = (f32[2880]{0:T(1024)S(1)}, f32[2880]{0:T(1024)}, u32[]{:S(2)}) copy-start(f32[2880]{0:T(1024)} %param.16) | copy-start | bytes 34564
  66.3 3.8 %collective-permute-start.3 = (bf16[4,16,2880]{2,1,0:T(8,128)(2,1)}, bf16[4,16,2880]{2,1,0:T(8,128)(2,1)S(1)}, u32[]{:S(2)}, u32[]{:S(2)}) collective-permute-start(bf16[4,16,2880]{2,1,0:T(8,128)(2,1)} %fusion.19), channel_id=1, source_target_pairs={{0,2},{2,0},{4,6},{6,4},{8,10},{10,8},{12,14},{14,12},{1,3},{3,1},... | collective-permute-start | bytes 1105928 | tf_op jit(solution)/shard_map/project/ppermute | solution.py:398
  70.9 17.4 %all-to-all-start.1 = ((bf16[4,16,2880]{2,1,0:T(8,128)(2,1)}), bf16[4,16,2880]{2,1,0:T(8,128)(2,1)S(1)}, u32[]{:S(2)}, u32[]{:S(2)}) async-start(bf16[4,16,2880]{2,1,0:T(8,128)(2,1)} %fusion.18), calls=%async_computation.1 | async-start | bytes 753664 | tf_op jit(solution)/shard_map/project/all_to_all | solution.py:401
Sparse Core Ops, SparseCore 0:
  10.5 138.6 all-gather.3
